TPU v7x, 256 devices: a whole 4x4x8 slice. The times are simulated.
256 devices in a mesh: scen: 8 (over y, core), tile: 32 (over z, x).
Axes of the slice: x: 4, y: 4, z: 8, core: 2. Of those that a mesh axis runs over, the one named last changes fastest.
Arguments:
- cotangent: float32 [32, 2, 8, 128, 512], P('scen', None, None, 'tile'), may hold values from -120 to 120
- scenario_ids: int32 [32], P('scen'), may hold values from 0 to 63
- weather: float32 [64, 8], replicated, may hold values from 0 to 2000, as said below
- landuse: int32 [128, 512], P('tile'), may hold values from 0 to 16
- class_diff: float32 [2, 17], replicated, may hold values from 0.5 to 4
- level_scale: float32 [8], replicated, may hold values from 0.6 to 1.6
- emit_profile: float32 [8], replicated, may hold values from 0.1 to 1
- building_cells: int32 [4096, 16], P('tile'), may hold values from 0 to 65535, as said below
Outputs:
- adjoint_state: float32 [32, 2, 8, 128, 512], P('scen', None, None, 'tile')
- control_grad: float32 [2, 4096], P(None, 'tile')
Inputs may be any that keep to these rules, and one draw needn't show every extreme that they name: `building_cells`: each building's cells form a 4 by 4 block of surface cells whose x rows lie in [k * 4, (k + 1) * 4) with k = b // 128; building 0 starts at cell 0 and the last building ends at the last cell. `weather`: rates along x and y lie in 100 to 2000, along z in 0.5 to 5, winds in 0 to 10, emission factors in 0.005 to 0.02.
All inputs are finite; a program needn't handle non-finite values.
Results may differ from a plain program's by a relative error of at most 0.0003.
Values sent between devices are 32-bit elements; how exact they have to be, the bound alone decides.
No kernel may reach another device: no remote copies, remote signals or barrier semaphores. Data moves between devices by JAX's collectives and lax.ppermute only.
A program may use at most 128 MiB of HBM per device.

v0:
```python
import math

import jax
import jax.numpy as jnp
from jax import lax
from jax.sharding import PartitionSpec as P


def extended(block, sides, width):
    for axis, dim in sides:
        count = lax.axis_size(axis)
        forward = [(i, i + 1) for i in range(count - 1)]
        backward = [(target, source) for source, target in forward]
        low = lax.ppermute(
            lax.slice_in_dim(block, block.shape[dim] - width, None, axis=dim), axis, forward
        )
        high = lax.ppermute(lax.slice_in_dim(block, 0, width, axis=dim), axis, backward)
        block = jnp.concatenate([low, block, high], axis=dim)
    return block


def adjoint_lines(cell_diff, rate, wind, axis):
    count = cell_diff.shape[axis]
    widths = [(0, 0)] * cell_diff.ndim
    widths[axis] = (1, 1)
    padded = jnp.pad(cell_diff, widths)
    left = (lax.slice_in_dim(padded, 0, count, axis=axis) + cell_diff) / 2.0
    right = (cell_diff + lax.slice_in_dim(padded, 2, count + 2, axis=axis)) / 2.0
    place = lax.broadcasted_iota(jnp.int32, cell_diff.shape, axis)
    lower = jnp.where(place > 0, -rate * left, 0.0 * left)
    upper = jnp.where(place < count - 1, -(rate * right + wind), 0.0 * right)
    middle = 1.0 + rate * (left + right) + wind
    return (lower, middle, upper)


def blocked_solve(lower, middle, upper, right_side):
    count = right_side.shape[0]
    depth = math.gcd(count, 16)
    groups = count // depth
    rest = right_side.shape[1:]

    def grouped(item):
        return item.reshape((groups, depth) + rest)

    def forward_block(carry, pieces):
        ratio_prev, value_prev = carry
        low, mid, upp, rhs = pieces
        ratios = []
        values = []
        for row in range(depth):
            denom = mid[row] - low[row] * ratio_prev
            value_prev = (rhs[row] - low[row] * value_prev) / denom
            ratio_prev = upp[row] / denom
            ratios.append(ratio_prev)
            values.append(value_prev)
        return ((ratio_prev, value_prev), (jnp.stack(ratios), jnp.stack(values)))

    zeros_rest = jnp.zeros(rest, jnp.float32)
    carried, stored = lax.scan(
        forward_block,
        (zeros_rest, zeros_rest),
        (grouped(lower), grouped(middle), grouped(upper), grouped(right_side)),
    )

    def backward_block(next_value, pieces):
        ratios, values = pieces
        outputs = [None] * depth
        for row in range(depth - 1, -1, -1):
            next_value = values[row] - ratios[row] * next_value
            outputs[row] = next_value
        return (next_value, jnp.stack(outputs))

    carried, solved = lax.scan(backward_block, zeros_rest, stored, reverse=True)
    return solved.reshape(right_side.shape)


def level_sweep(lower, middle, upper, right_side):
    shape = right_side.shape
    lower = jnp.broadcast_to(lower, shape)
    middle = jnp.broadcast_to(middle, shape)
    upper = jnp.broadcast_to(upper, shape)
    levels = shape[2]
    ratios = []
    values = []
    for level in range(levels):
        if level == 0:
            denom = middle[:, :, 0]
            values.append(right_side[:, :, 0] / denom)
        else:
            denom = middle[:, :, level] - lower[:, :, level] * ratios[-1]
            values.append((right_side[:, :, level] - lower[:, :, level] * values[-1]) / denom)
        ratios.append(upper[:, :, level] / denom)
    result = [values[-1]]
    for level in range(levels - 2, -1, -1):
        result.append(values[level] - ratios[level] * result[-1])
    return jnp.stack(result[::-1], axis=2)


def slab_sweep(lower, middle, upper, right_side, couple_first, couple_last):
    rows = right_side.shape[3]
    denoms = []
    ratios = []
    for row in range(rows):
        if row == 0:
            denom = middle[:, :, :, 0]
        else:
            denom = middle[:, :, :, row] - lower[:, :, :, row] * ratios[-1]
        denoms.append(denom)
        ratios.append(upper[:, :, :, row] / denom)
    main_fwd = []
    first_fwd = []
    for row in range(rows):
        if row == 0:
            main_fwd.append(right_side[:, :, :, 0] / denoms[0])
            first_fwd.append(couple_first / denoms[0])
        else:
            main_fwd.append(
                (right_side[:, :, :, row] - lower[:, :, :, row] * main_fwd[-1]) / denoms[row]
            )
            first_fwd.append(-lower[:, :, :, row] * first_fwd[-1] / denoms[row])
    last_top = couple_last / denoms[rows - 1]
    main_out = [main_fwd[-1]]
    first_out = [first_fwd[-1]]
    last_out = [last_top]
    for row in range(rows - 2, -1, -1):
        main_out.append(main_fwd[row] - ratios[row] * main_out[-1])
        first_out.append(first_fwd[row] - ratios[row] * first_out[-1])
        last_out.append(-ratios[row] * last_out[-1])
    return (
        jnp.stack(main_out[::-1], axis=3),
        jnp.stack(first_out[::-1], axis=3),
        jnp.stack(last_out[::-1], axis=3),
    )


def on_device(
    cotangent, scenario_ids, weather, landuse, class_diff, level_scale, emit_profile, building_cells
):
    scen_local = cotangent.shape[0]
    slab_rows = cotangent.shape[3]
    width_y = cotangent.shape[4]
    pick = (scenario_ids[:, None] == jnp.arange(weather.shape[0], dtype=jnp.int32)[None, :]).astype(
        jnp.float32
    )
    table = jnp.sum(pick[:, :, None] * weather[None], axis=1)
    marks = (
        landuse[None] == jnp.arange(class_diff.shape[1], dtype=jnp.int32)[:, None, None]
    ).astype(jnp.float32)
    surface = jnp.sum(class_diff[:, :, None, None] * marks[None], axis=1)
    cell_diff = surface[:, None] * level_scale[None, :, None, None]

    def column_of(index):
        return table[:, index].reshape(scen_local, 1, 1, 1, 1)

    lower, middle, upper = adjoint_lines(cell_diff, column_of(2), column_of(5), 1)
    field = level_sweep(lower, middle, upper, cotangent)
    lower, middle, upper = adjoint_lines(cell_diff, column_of(1), column_of(4), 3)
    full_shape = field.shape

    def to_lines(item):
        return jnp.moveaxis(jnp.broadcast_to(item, full_shape), 4, 0).reshape(width_y, -1)

    solved_y = blocked_solve(to_lines(lower), to_lines(middle), to_lines(upper), to_lines(field))
    field = jnp.moveaxis(solved_y.reshape((width_y,) + full_shape[:4]), 0, 4)
    rate_x = column_of(0)
    wind_x = column_of(3)
    padded = extended(cell_diff, (("tile", 2),), 1)
    left = (padded[:, :, :-2] + cell_diff) / 2.0
    right = (cell_diff + padded[:, :, 2:]) / 2.0
    lower = -rate_x * left
    upper = -(rate_x * right + wind_x)
    middle = 1.0 + rate_x * (left + right) + wind_x
    couple_first = lower[:, :, :, 0]
    couple_last = upper[:, :, :, -1]
    row_place = lax.broadcasted_iota(jnp.int32, lower.shape, 3)
    lower = jnp.where(row_place > 0, lower, 0.0)
    upper = jnp.where(row_place < slab_rows - 1, upper, 0.0)
    local_value, from_left, from_right = slab_sweep(
        lower, middle, upper, field, couple_first, couple_last
    )
    ends = (
        lax.all_gather(local_value[:, :, :, 0:1], "tile", axis=3, tiled=True),
        lax.all_gather(local_value[:, :, :, slab_rows - 1 : slab_rows], "tile", axis=3, tiled=True),
        lax.all_gather(from_left[:, :, :, 0:1], "tile", axis=3, tiled=True),
        lax.all_gather(from_left[:, :, :, slab_rows - 1 : slab_rows], "tile", axis=3, tiled=True),
        lax.all_gather(from_right[:, :, :, 0:1], "tile", axis=3, tiled=True),
        lax.all_gather(from_right[:, :, :, slab_rows - 1 : slab_rows], "tile", axis=3, tiled=True),
    )
    value_first, value_last, left_first, left_last, right_first, right_last = [
        jnp.moveaxis(item, 3, 0) for item in ends
    ]

    def forward_step(carry, slices):
        carry_ratio, carry_value = carry
        v_first, v_last, f_first, f_last, g_first, g_last = slices
        denom = 1.0 - f_first * carry_ratio
        coef_first = g_first / denom
        coef_last = g_last + f_last * carry_ratio * g_first / denom
        rest_first = v_first - f_first * carry_value
        rest_last = v_last - f_last * carry_value
        sol_first = rest_first / denom
        sol_last = rest_last + f_last * carry_ratio * rest_first / denom
        return ((coef_last, sol_last), (coef_first, coef_last, sol_first, sol_last))

    zeros_plane = jnp.zeros(value_first.shape[1:], jnp.float32)
    carried, reduced = lax.scan(
        forward_step,
        (zeros_plane, zeros_plane),
        (value_first, value_last, left_first, left_last, right_first, right_last),
    )

    def backward_step(next_first, slices):
        coef_first, coef_last, sol_first, sol_last = slices
        this_first = sol_first - coef_first * next_first
        this_last = sol_last - coef_last * next_first
        return (this_first, (this_first, this_last))

    carried, bounds = lax.scan(backward_step, zeros_plane, reduced, reverse=True)
    firsts, lasts = bounds
    position = lax.axis_index("tile")
    count = lax.axis_size("tile")
    prev_last = jnp.where(
        position > 0,
        lax.dynamic_index_in_dim(lasts, jnp.maximum(position - 1, 0), 0, keepdims=False),
        zeros_plane,
    )
    next_first = jnp.where(
        position < count - 1,
        lax.dynamic_index_in_dim(firsts, jnp.minimum(position + 1, count - 1), 0, keepdims=False),
        zeros_plane,
    )
    adjoint_state = (
        local_value - prev_last[:, :, :, None] * from_left - next_first[:, :, :, None] * from_right
    )
    column = jnp.sum(adjoint_state * emit_profile[None, None, :, None, None], axis=2)
    column = column.reshape(scen_local, 2, slab_rows * width_y)
    local_index = (building_cells - lax.axis_index("tile") * slab_rows * width_y).reshape(-1)
    picked = jnp.take(column, local_index, axis=2)
    buildings = building_cells.shape[0]
    per_building = jnp.sum(
        picked.reshape(scen_local, 2, buildings, building_cells.shape[1]), axis=3
    )
    partial_grad = jnp.sum(per_building * table[:, 6:8, None], axis=0)
    control_grad = lax.psum(partial_grad, "scen")
    return (adjoint_state, control_grad)


def solution(mesh):
    placed = (
        P("scen", None, None, "tile", None),
        P("scen"),
        P(),
        P("tile", None),
        P(),
        P(),
        P(),
        P("tile", None),
    )
    return jax.shard_map(
        on_device,
        mesh=mesh,
        in_specs=placed,
        out_specs=(P("scen", None, None, "tile", None), P(None, "tile")),
        check_vma=False,
    )
```

profile of v0, /device:TPU:1, one launch (start us, length us, event | category | flops | bytes accessed | tf_op | source)
XLA Modules:
  0.0 963.9 jit_solution(13469782934922088242)
XLA Ops:
  9.5 3.9 collective-permute-start
  34.9 3.5 copy.124
  38.7 2.8 broadcast_in_dim.131
  45.4 2.7 mul.862
  48.2 7.7 add_add_fusion
  55.9 4.3 copy.121
  60.2 4.3 copy.122
  64.6 2.8 broadcast_in_dim.135
  70.3 6.0 multiply_select_fusion
  76.3 4.3 copy.123
  82.3 142.1 %while.74 = (s32[]{:T(128)}, f32[256]{0:T(256)S(1)}, f32[256]{0:T(256)S(1)}, f32[32,16,256]{2,1,0:T(8,128)}, f32[32,16,256]{2,1,0:T(8,128)}, /*index=5*/f32[32,1...) while((s32[]{:T(128)}, f32[256]{0:T(256)S(1)}, ...), condition=%wide.region_3.4_spmd.clone, body=%wide.region_2.3_spmd.clone.sunk | while | flops 25618 | bytes 366755 | solution.py:59
  224.4 52.3 %while.75 = (s32[]{:T(128)}, f32[256]{0:T(256)S(1)}, f32[32,16,256]{2,1,0:T(8,128)S(1)}, f32[32,16,256]{2,1,0:T(8,128)}, f32[32,16,256]{2,1,0:T(8,128)}, /*index...) while((s32[]{:T(128)}, f32[256]{0:T(256)S(1)}, ...), condition=%wide.region_5.6_spmd.clone, body=%wide.region_4.5_spmd.clone.sunk | while | flops 8467 | bytes 181723 | solution.py:73
  276.7 4.4 copy.125
  281.0 3.8 reshape_reshape.10
  291.5 80.9 %all-gather.9.cloned.1.call-done = f32[4,2,8,32,512]{4,2,1,0,3:T(8,128)} async-done(((f32[4,2,8,1,512]{4,2,1,0,3:T(8,128)}), f32[4,2,8,32,512]{4,2,1,0,3:T(8,128)}) %all-gather.9.cloned.1.call-update) | async-done | bytes 4194320 | tf_op jit(solution)/shard_map/all_gather | solution.py:185
  372.4 81.8 %all-gather.13.cloned.1.call-done = f32[4,2,8,32,512]{4,2,1,0,3:T(8,128)} async-done(((f32[4,2,8,1,512]{4,2,1,0,3:T(8,128)}), f32[4,2,8,32,512]{4,2,1,0,3:T(8,128)}) %all-gather.13.cloned.1.call-update) | async-done | bytes 4194320 | tf_op jit(solution)/shard_map/all_gather | solution.py:184
  454.2 81.8 %all-gather.15.cloned.1.call-done = f32[4,2,8,32,512]{4,2,1,0,3:T(8,128)} async-done(((f32[4,2,8,1,512]{4,2,1,0,3:T(8,128)}), f32[4,2,8,32,512]{4,2,1,0,3:T(8,128)}) %all-gather.15.cloned.1.call-update) | async-done | bytes 4194320 | tf_op jit(solution)/shard_map/all_gather | solution.py:183
  536.0 82.2 %all-gather.17.cloned.1.call-done = f32[4,2,8,32,512]{4,2,1,0,3:T(8,128)} async-done(((f32[4,2,8,1,512]{4,2,1,0,3:T(8,128)}), f32[4,2,8,32,512]{4,2,1,0,3:T(8,128)}) %all-gather.17.cloned.1.call-update) | async-done | bytes 4194320 | tf_op jit(solution)/shard_map/all_gather | solution.py:182
  618.2 81.6 %all-gather.11.cloned.1.call-done = f32[4,2,8,32,512]{4,2,1,0,3:T(8,128)} async-done(((f32[4,2,8,1,512]{4,2,1,0,3:T(8,128)}), f32[4,2,8,32,512]{4,2,1,0,3:T(8,128)}) %all-gather.11.cloned.1.call-update) | async-done | bytes 4194320 | tf_op jit(solution)/shard_map/all_gather | solution.py:186
  699.8 81.6 %all-gather.7.cloned.1.call-done = f32[4,2,8,32,512]{4,2,1,0,3:T(8,128)} async-done(((f32[4,2,8,1,512]{4,2,1,0,3:T(8,128)}), f32[4,2,8,32,512]{4,2,1,0,3:T(8,128)}) %all-gather.7.cloned.1.call-update) | async-done | bytes 4194320 | tf_op jit(solution)/shard_map/all_gather | solution.py:187
  791.6 67.3 %while.76 = (s32[]{:T(128)}, f32[4,2,8,512]{3,2,1,0:T(8,128)S(1)}, f32[4,2,8,512]{3,2,1,0:T(8,128)S(1)}, f32[32,4,2,8,512]{4,3,2,1,0:T(8,128)}, f32[32,4,2,8,512...) while((s32[]{:T(128)}, f32[4,2,8,512]{3,2,1,0:T(8,128)S(1)}, ...), condition=%wide.region_7.8_spmd.clone, body=%wide.region_6.7_spmd.clone.sunk | while | flops 557059 | bytes 1835671 | solution.py:206
  864.0 60.7 %while.77 = (s32[]{:T(128)}, f32[4,2,8,512]{3,2,1,0:T(8,128)S(1)}, f32[32,4,2,8,512]{4,3,2,1,0:T(8,128)}, f32[32,4,2,8,512]{4,3,2,1,0:T(8,128)}, f32[32,4,2,8,51...) while((s32[]{:T(128)}, f32[4,2,8,512]{3,2,1,0:T(8,128)S(1)}, ...), condition=%wide.region_9.10_spmd.clone, body=%wide.region_8.9_spmd.clone.sunk | while | flops 163844 | bytes 1048711 | solution.py:218
  929.3 8.4 gather_fusion
  940.3 15.6 %psum.7 = f32[2,128]{1,0:T(2,128)} all-reduce(f32[2,128]{1,0:T(2,128)S(1)} %multiply_reduce_fusion.3), channel_id=1, replica_groups=mesh['scen'=8,'tile'=32] {'scen'}, use_global_device_ids=true, to_apply=%region_13.14 | all-reduce | flops 256 | bytes 2048 | tf_op jit(solution)/shard_map/psum | solution.py:244
  (603 shorter events, 382.4 us)
Async XLA Ops:
  7.2 365.2 %all-gather.9.cloned.1.call-start = ((), (), s32[]{:S(2)}) async-start(), calls=%async_computation.1 | async-start | bytes 4325376 | tf_op jit(solution)/shard_map/all_gather | solution.py:185
  9.5 13.8 %collective-permute-start = (f32[2,8,1,512]{3,1,2,0:T(8,128)S(1)}, f32[2,8,1,512]{3,1,2,0:T(8,128)S(1)}, u32[]{:S(2)}, u32[]{:S(2)}) collective-permute-start(f32[2,8,1,512]{3,1,2,0:T(8,128)S(1)} %get-tuple-element.937), channel_id=1, source_target_pairs={{0,1},{1,2},{2,3},{3,4},{4,5},{5,6},{6,7},{7,8},{8,9},{9,10},{10,1... | collective-permute-start | bytes 98312 | tf_op jit(solution)/shard_map/ppermute | solution.py:14
  13.5 9.9 %collective-permute-start.1 = (f32[2,8,1,512]{3,1,2,0:T(8,128)S(1)}, f32[2,8,1,512]{3,1,2,0:T(8,128)S(1)}, u32[]{:S(2)}, u32[]{:S(2)}) collective-permute-start(f32[2,8,1,512]{3,1,2,0:T(8,128)S(1)} %get-tuple-element.938), channel_id=1, source_target_pairs={{1,0},{2,1},{3,2},{4,3},{5,4},{6,5},{7,6},{8,7},{9,8},{10,9},{11,1... | collective-permute-start | bytes 98312 | tf_op jit(solution)/shard_map/ppermute | solution.py:17
  19.3 1.8 copy-start.12
  19.3 1.8 copy-start.13
  25.1 3.1 copy-start.7
  25.1 3.9 copy-start.8
  34.9 3.6 copy-start.6
  64.6 5.7 copy-start.9
  64.6 5.7 copy-start.11
  285.0 6.2 copy-start.10
  287.8 166.3 %all-gather.13.cloned.1.call-start = ((), (), s32[]{:S(2)}) async-start(), calls=%async_computation.3 | async-start | bytes 4325376 | tf_op jit(solution)/shard_map/all_gather | solution.py:184
  288.6 247.4 %all-gather.15.cloned.1.call-start = ((), (), s32[]{:S(2)}) async-start(), calls=%async_computation.4 | async-start | bytes 4325376 | tf_op jit(solution)/shard_map/all_gather | solution.py:183
  289.3 328.8 %all-gather.17.cloned.1.call-start = ((), (), s32[]{:S(2)}) async-start(), calls=%async_computation.5 | async-start | bytes 4325376 | tf_op jit(solution)/shard_map/all_gather | solution.py:182
  289.9 409.9 %all-gather.11.cloned.1.call-start = ((), (), s32[]{:S(2)}) async-start(), calls=%async_computation.2 | async-start | bytes 4325376 | tf_op jit(solution)/shard_map/all_gather | solution.py:186
  290.5 490.9 %all-gather.7.cloned.1.call-start = ((), (), s32[]{:S(2)}) async-start(), calls=%async_computation | async-start | bytes 4325376 | tf_op jit(solution)/shard_map/all_gather | solution.py:187
  861.4 65.2 %copy-start = (f32[4,2,8,1,512]{4,2,3,1,0:T(8,128)S(1)}, f32[4,2,8,1,512]{4,2,3,1,0:T(8,128)}, u32[]{:S(2)}) copy-start(f32[4,2,8,1,512]{4,2,3,1,0:T(8,128)} %get-tuple-element.748) | copy-start | bytes 393220
  861.4 65.2 %copy-start.1 = (f32[4,2,8,1,512]{4,2,3,1,0:T(8,128)S(1)}, f32[4,2,8,1,512]{4,2,3,1,0:T(8,128)}, u32[]{:S(2)}) copy-start(f32[4,2,8,1,512]{4,2,3,1,0:T(8,128)} %get-tuple-element.751) | copy-start | bytes 393220
  861.4 65.2 %copy-start.2 = (f32[4,2,8,1,512]{4,2,3,1,0:T(8,128)S(1)}, f32[4,2,8,1,512]{4,2,3,1,0:T(8,128)}, u32[]{:S(2)}) copy-start(f32[4,2,8,1,512]{4,2,3,1,0:T(8,128)} %get-tuple-element.907) | copy-start | bytes 393220
  861.4 65.2 %copy-start.3 = (f32[4,2,8,1,512]{4,2,3,1,0:T(8,128)S(1)}, f32[4,2,8,1,512]{4,2,3,1,0:T(8,128)}, u32[]{:S(2)}) copy-start(f32[4,2,8,1,512]{4,2,3,1,0:T(8,128)} %get-tuple-element.910) | copy-start | bytes 393220
  861.4 65.2 %copy-start.4 = (f32[4,2,8,1,512]{4,2,3,1,0:T(8,128)S(1)}, f32[4,2,8,1,512]{4,2,3,1,0:T(8,128)}, u32[]{:S(2)}) copy-start(f32[4,2,8,1,512]{4,2,3,1,0:T(8,128)} %get-tuple-element.734) | copy-start | bytes 393220
  861.4 65.2 %copy-start.5 = (f32[4,2,8,1,512]{4,2,3,1,0:T(8,128)S(1)}, f32[4,2,8,1,512]{4,2,3,1,0:T(8,128)}, u32[]{:S(2)}) copy-start(f32[4,2,8,1,512]{4,2,3,1,0:T(8,128)} %get-tuple-element.737) | copy-start | bytes 393220
  861.4 65.2 %copy-start.14 = (f32[8]{0:T(128)S(1)}, f32[8]{0:T(128)}, u32[]{:S(2)}) copy-start(f32[8]{0:T(128)} %param.22) | copy-start | bytes 100
Sparse Core Ops, SparseCore 0:
  288.0 84.3 all-gather.8
  375.0 79.1 all-gather.12
  456.8 79.1 all-gather.14
  539.0 79.1 all-gather.16
  620.6 79.1 all-gather.10
  702.2 79.1 all-gather.6
where the time goes:
time: 974 us; the launch traced here: 964 us
  waiting for transfers between devices  493 us (51%)
  local copies, waits for them, and re-layouts  258 us (26%)
  other arithmetic  175 us (18%)
  blocking collectives  15.6 us (2%)
  between operations  14.6 us (1%)
    dynamic_update_slice x64, other arithmetic, on_device(): lax.scan(forward_step, (zeros_plane, zeros_plane), (value_first, value_la...  128 us
    all_gather x1, waiting for transfers between devices, on_device(): lax.all_gather(local_value[:, :, :, 0:1], 'tile', axis=3, tiled=True)  82.2 us
    all_gather x1, waiting for transfers between devices, on_device(): lax.all_gather(local_value[:, :, :, slab_rows - 1:slab_rows], 'tile', axi...  81.8 us
    all_gather x1, waiting for transfers between devices, on_device(): lax.all_gather(from_left[:, :, :, 0:1], 'tile', axis=3, tiled=True)  81.8 us
    all_gather x1, waiting for transfers between devices, on_device(): lax.all_gather(from_right[:, :, :, slab_rows - 1:slab_rows], 'tile', axis...  81.6 us
    all_gather x1, waiting for transfers between devices, on_device(): lax.all_gather(from_right[:, :, :, 0:1], 'tile', axis=3, tiled=True)  81.6 us
    all_gather x1, waiting for transfers between devices, on_device(): lax.all_gather(from_left[:, :, :, slab_rows - 1:slab_rows], 'tile', axis=...  80.9 us
    slice x64, local copies, waits for them, and re-layouts, forward_block(): denom = mid[row] - low[row] * ratio_prev  67.8 us
  transfers between devices with their start and end apart: 8, of which 6 were waited for; matrix products, arithmetic and copies ran while one was open for 1% of the time, Pallas kernels for 0%

commit v1 on v0

v1 whole, which is shorter than its diff:
```python
import jax
import jax.numpy as jnp
from jax import lax
from jax.experimental import pallas as pl
from jax.experimental.pallas import tpu as pltpu
from jax.sharding import PartitionSpec as P

F32 = jnp.float32
SEND = 24


def inverse(value):
    guess = pl.reciprocal(value, approx=True)
    guess = guess * (2.0 - value * guess)
    return guess * (2.0 - value * guess)


def sublane():
    return lax.broadcasted_iota(jnp.int32, (8, 128), 0)


def lane():
    return lax.broadcasted_iota(jnp.int32, (8, 128), 1)


def choose(index, values):
    out = jnp.full((8, 128), values[-1], F32)
    for at in range(len(values) - 2, -1, -1):
        out = jnp.where(index == at, values[at], out)
    return out


def surface(classes, class_diff, field):
    out = jnp.zeros((8, 128), F32)
    for mark in range(class_diff.shape[1]):
        out = jnp.where(classes == mark, class_diff[field, mark], out)
    return out


def swap_halves(value):
    return pltpu.roll(value, 4, axis=0)


def pair_halves(first, second, low):
    return (
        jnp.where(low, first, swap_halves(second)),
        jnp.where(low, swap_halves(first), second),
    )


def solve_levels(cot, surf, scale, table, out, hold_a, hold_c, low):
    half = [(scale[z] + scale[z + 1]) * 0.5 for z in range(7)]
    for pair in range(2):
        chains = [(s, f, h) for s in (2 * pair, 2 * pair + 1) for f in range(2) for h in range(2)]
        rated = [surf[f][h] * table(s, 2) for s, f, h in chains]
        winds = [table(s, 5) for s, f, h in chains]
        values = [None] * 8
        slacks = [None] * 8
        faces = [None] * 8
        for z in range(8):
            for n, (s, f, h) in enumerate(chains):
                rhs = cot[pl.ds(s * 256 + f * 128 + z * 16 + h * 8, 8), :]
                if z == 0:
                    slack = 1.0 + rated[n] * (scale[0] * 0.5)
                else:
                    slack = 1.0 + faces[n] * slacks[n]
                    rhs = rhs + faces[n] * values[n]
                if z < 7:
                    face = rated[n] * half[z]
                    above = face + winds[n]
                    inv = inverse(above + slack)
                    values[n] = rhs * inv
                    slacks[n] = slack * inv
                    faces[n] = face
                    hold_a[pl.ds((z * 8 + n) * 8, 8), :] = values[n]
                    hold_c[pl.ds((z * 8 + n) * 8, 8), :] = above * inv
                else:
                    slack = slack + (rated[n] * (scale[7] * 0.5) + winds[n])
                    values[n] = rhs * inverse(slack)
        for z in range(7, -1, -1):
            if z < 7:
                for n in range(8):
                    at = pl.ds((z * 8 + n) * 8, 8)
                    values[n] = hold_a[at, :] + hold_c[at, :] * values[n]
            for f in range(2):
                for h in range(2):
                    n = f * 2 + h
                    even, odd = pair_halves(values[n], values[n + 4], low)
                    for yb, item in ((2 * h, even), (2 * h + 1, odd)):
                        out[pl.ds((f * 4 + yb) * 128 + z * 16 + pair * 8, 8), :] = item


def from_before(items, rows, distance):
    turned = [pltpu.roll(item, distance, axis=0) for item in items]
    return [
        turned[v] if v % 4 == 0 else jnp.where(rows < distance, turned[v - 1], turned[v])
        for v in range(8)
    ]


def from_after(items, rows, distance):
    turned = [pltpu.roll(item, 8 - distance, axis=0) for item in items]
    return [
        turned[v] if v % 4 == 3 else jnp.where(rows >= 8 - distance, turned[v + 1], turned[v])
        for v in range(8)
    ]


def solve_chunks(below, above, slack, rhs, rows):
    everyone = range(8)
    for distance in (1, 2, 4, 8, 16):
        inv = [inverse(below[v] + above[v] + slack[v]) for v in everyone]
        nb = [below[v] * inv[v] for v in everyone]
        na = [above[v] * inv[v] for v in everyone]
        ns = [slack[v] * inv[v] for v in everyone]
        nr = [rhs[v] * inv[v] for v in everyone]
        new_slack = list(slack)
        new_rhs = list(rhs)
        if distance < 8:
            pb, ps, pr = (from_before(item, rows, distance) for item in (nb, ns, nr))
            qa, qs, qr = (from_after(item, rows, distance) for item in (na, ns, nr))
            has_before = has_after = [True] * 8
        else:
            jump = distance // 8
            has_before = [v % 4 >= jump for v in everyone]
            has_after = [v % 4 < 4 - jump for v in everyone]
            pb, ps, pr = (
                [item[v - jump] if has_before[v] else None for v in everyone]
                for item in (nb, ns, nr)
            )
            qa, qs, qr = (
                [item[v + jump] if has_after[v] else None for v in everyone]
                for item in (na, ns, nr)
            )
        zero = jnp.zeros((8, 128), F32)
        new_below = [zero] * 8
        new_above = [zero] * 8
        for v in everyone:
            if has_before[v]:
                new_slack[v] = new_slack[v] + below[v] * ps[v]
                new_rhs[v] = new_rhs[v] + below[v] * pr[v]
                new_below[v] = below[v] * pb[v]
            if has_after[v]:
                new_slack[v] = new_slack[v] + above[v] * qs[v]
                new_rhs[v] = new_rhs[v] + above[v] * qr[v]
                new_above[v] = above[v] * qa[v]
        below, above, slack, rhs = new_below, new_above, new_slack, new_rhs
    return [rhs[v] * inverse(slack[v]) for v in everyone]


def solve_rows(turned, faces, leak, rate, wind, hold_a, hold_b, hold_c, rows):
    everyone = range(8)
    depth = 16

    def at(v, i):
        return pl.ds(v * 128 + i, 8, stride=depth)

    def keep(i, v):
        return pl.ds((i * 8 + v) * 8, 8)

    ends = [faces[at(v, depth - 1), :] * rate for v in everyone]
    before = from_before(ends, rows, 1)
    last = ends
    value = [None] * 8
    fill = [None] * 8
    slack = [None] * 8
    for i in range(depth):
        for v in everyone:
            rhs = turned[at(v, i), :]
            face = last[v] if i == depth - 1 else faces[at(v, i), :] * rate
            next_coef = face + wind
            if i == 0:
                link = before[v]
                own = jnp.ones((8, 128), F32)
                if v % 4 == 0:
                    own = jnp.where(rows == 0, 1.0 + leak[v // 4], own)
                    link = jnp.where(rows == 0, 0.0, link)
            else:
                link = before[v] * fill[v]
                own = 1.0 + before[v] * slack[v]
                rhs = rhs + before[v] * value[v]
            if i == depth - 1:
                if v % 4 == 3:
                    own = jnp.where(rows == 7, own + next_coef, own)
                    next_coef = jnp.where(rows == 7, 0.0, next_coef)
                value[v], fill[v], slack[v] = rhs, link, own
                before[v] = next_coef
                continue
            inv = inverse(next_coef + link + own)
            value[v] = rhs * inv
            fill[v] = link * inv
            slack[v] = own * inv
            upper = next_coef * inv
            hold_a[keep(i, v), :] = value[v]
            hold_b[keep(i, v), :] = fill[v]
            hold_c[keep(i, v), :] = upper
            before[v] = face
            if i == 0:
                if v == 0:
                    first_value, first_fill, first_slack, first_next = ([None] * 8 for _ in range(4))
                first_value[v], first_fill[v], first_slack[v], first_next[v] = (
                    value[v],
                    fill[v],
                    slack[v],
                    upper,
                )
            else:
                carry = first_next[v]
                first_value[v] = first_value[v] + carry * value[v]
                first_slack[v] = first_slack[v] + carry * slack[v]
                first_next[v] = carry * upper
    next_value = from_after(first_value, rows, 1)
    next_slack = from_after(first_slack, rows, 1)
    next_next = from_after(first_next, rows, 1)
    above = [before[v] * next_next[v] for v in everyone]
    slack = [slack[v] + before[v] * next_slack[v] for v in everyone]
    rhs = [value[v] + before[v] * next_value[v] for v in everyone]
    current = solve_chunks(fill, above, slack, rhs, rows)
    previous = from_before(current, rows, 1)
    for v in everyone:
        turned[at(v, depth - 1), :] = current[v]
    for i in range(depth - 2, -1, -1):
        for v in everyone:
            item = hold_a[keep(i, v), :] + hold_b[keep(i, v), :] * previous[v]
            current[v] = item + hold_c[keep(i, v), :] * current[v]
            turned[at(v, i), :] = current[v]


def inner_coefs(low_face, mid_face, high_face, wind):
    one_next = mid_face + wind
    one_inv = inverse(low_face + one_next + 1.0)
    one_fill = low_face * one_inv
    one_upper = one_next * one_inv
    two_next = high_face + wind
    two_fill = mid_face * one_fill
    two_slack = 1.0 + mid_face * one_inv
    two_inv = inverse(two_next + two_fill + two_slack)
    return one_inv, one_fill, one_upper, two_inv, two_fill, two_slack, two_next


def first_kernel(
    ids, weather, class_diff, scale, cot, landuse, sent, kept,
    levels, turned, faces, hold_a, hold_b, hold_c, surf_rows,
):
    rows = sublane()
    lanes = lane()
    low = rows < 4

    def table(s, column):
        return weather[ids[s], column]

    classes = [landuse[pl.ds(0, 8), :], landuse[pl.ds(8, 8), :]]
    surf = [[surface(item, class_diff, f) for item in classes] for f in range(2)]
    rate_y = choose((lanes // 4) % 4, [table(s, 1) for s in range(4)])
    wind_y = choose((lanes // 4) % 4, [table(s, 4) for s in range(4)])
    rate_y = rate_y * choose(lanes // 16, [scale[z] for z in range(8)])
    leak = []
    for f in range(2):
        upper, lower = surf[f]
        surf_rows[pl.ds(f * 16, 8), :] = upper
        surf_rows[pl.ds(f * 16 + 8, 8), :] = lower
        shifted = [pltpu.roll(item, 127, axis=1) for item in (upper, lower)]
        swapped = [swap_halves(item) for item in shifted]
        onward = [
            jnp.where(low, swapped[0], swapped[1]),
            jnp.where(low, swapped[1], 0.0),
        ]
        for h in range(2):
            right = jnp.where(lanes == 127, onward[h], shifted[h])
            face = (surf[f][h] + right) * 0.5
            other = swap_halves(face)
            for yb, item in (
                (2 * h, jnp.where(low, face, other)),
                (2 * h + 1, jnp.where(low, other, face)),
            ):
                tile = jnp.concatenate([item] * 16, axis=0)
                faces[pl.ds((f * 4 + yb) * 128, 128), :] = tile.T
        start = jnp.broadcast_to(upper[:, 0:1], (8, 128))
        start = jnp.where(rows == lanes % 4, start, 0.0)
        start = jnp.broadcast_to(jnp.sum(start, axis=0, keepdims=True), (8, 128))
        leak.append(start * 0.5 * rate_y)

    solve_levels(cot, surf, scale, table, levels, hold_a, hold_c, low)
    for v in range(8):
        block = pl.ds(v * 128, 128)
        turned[block, :] = levels[block, :].T
    solve_rows(turned, faces, leak, rate_y, wind_y, hold_a, hold_b, hold_c, rows)
    for v in range(8):
        block = pl.ds(v * 128, 128)
        levels[block, :] = turned[block, :].T

    rate_x = choose(rows % 4, [table(s, 0) for s in range(4)])
    wind_x = choose(rows % 4, [table(s, 3) for s in range(4)])
    for v in range(8):
        line = [surf_rows[pl.ds(v * 4 + x, 1), :] for x in range(4)]
        steps = [(line[x] + line[x + 1]) * 0.5 for x in range(3)]
        four = surf_rows[pl.ds((v // 2) * 8, 8), :]
        for zp in range(4):
            j = v * 4 + zp
            rate = rate_x * choose(rows // 4, [scale[2 * zp], scale[2 * zp + 1]])
            e01, e12, e23 = (rate * step for step in steps)
            rhs = [levels[pl.ds(v * 128 + zp * 32 + x, 8, stride=4), :] for x in range(4)]
            one_inv, one_fill, one_upper, two_inv, two_fill, two_slack, two_next = inner_coefs(
                e01, e12, e23, wind_x
            )
            one = rhs[1] * one_inv
            two = (rhs[2] + e12 * one) * two_inv
            sent[j, pl.ds(0, 8), :] = rhs[0] + (e01 + wind_x) * (one + one_upper * two)
            sent[j, pl.ds(8, 8), :] = rhs[3] + e23 * two
            sent[j, pl.ds(16, 8), :] = four if v % 2 == 0 else swap_halves(four)
            for n, item in enumerate(
                (one, one_fill, one_upper, two, two_fill * two_inv, two_next * two_inv)
            ):
                kept[j, pl.ds(n * 8, 8), :] = item


def middle_kernel(place, ids, weather, scale, got, ends):
    rows = sublane()

    def table(s, column):
        return weather[ids[s], column]

    rate = choose(rows % 4, [table(s, 0) for s in range(4)])
    wind = choose(rows % 4, [table(s, 3) for s in range(4)])
    zp = place[0] % 4
    rate = rate * choose(rows // 4, [scale[2 * zp], scale[2 * zp + 1]])
    slabs = got.shape[0]
    below, above, slack, rhs = [], [], [], []
    line = None
    outer = None
    for k in range(slabs):
        line = [got[k, pl.ds(16 + x, 1), :] for x in range(4)]
        if k == 0:
            outer = rate * (line[0] * 0.5)
        e01, e12, e23 = (rate * ((line[x] + line[x + 1]) * 0.5) for x in range(3))
        one_inv, one_fill, one_upper, two_inv, two_fill, two_slack, two_next = inner_coefs(
            e01, e12, e23, wind
        )
        two_slack = two_slack * two_inv
        q0 = e01 + wind
        own = 1.0 + q0 * (one_inv + one_upper * two_slack)
        if k == 0:
            own = own + outer
            below.append(None)
        else:
            below.append(outer)
        above.append(q0 * (one_upper * (two_next * two_inv)))
        slack.append(own)
        rhs.append(got[k, pl.ds(0, 8), :])
        if k < slabs - 1:
            outer = rate * ((line[3] + got[k + 1, pl.ds(16, 1), :]) * 0.5)
        else:
            outer = rate * (line[3] * 0.5)
        own = 1.0 + e23 * two_slack
        below.append(e23 * (two_fill * two_inv))
        if k < slabs - 1:
            above.append(outer + wind)
        else:
            own = own + (outer + wind)
            above.append(None)
        slack.append(own)
        rhs.append(got[k, pl.ds(8, 8), :])

    def total(i):
        out = slack[i]
        if below[i] is not None:
            out = out + below[i]
        if above[i] is not None:
            out = out + above[i]
        return out

    count = 2 * slabs
    alive = list(range(count))
    removed = []
    while len(alive) > 1:
        gone = alive[1::2]
        stay = alive[0::2]
        normal = {}
        for i in gone:
            inv = inverse(total(i))
            normal[i] = (
                below[i] * inv,
                None if above[i] is None else above[i] * inv,
                slack[i] * inv,
                rhs[i] * inv,
            )
        for n, i in enumerate(stay):
            new_below = new_above = None
            new_slack, new_rhs = slack[i], rhs[i]
            if n > 0:
                nb, na, ns, nr = normal[gone[n - 1]]
                new_slack = new_slack + below[i] * ns
                new_rhs = new_rhs + below[i] * nr
                new_below = below[i] * nb
            if n < len(gone):
                nb, na, ns, nr = normal[gone[n]]
                new_slack = new_slack + above[i] * ns
                new_rhs = new_rhs + above[i] * nr
                new_above = None if na is None else above[i] * na
            below[i], above[i], slack[i], rhs[i] = new_below, new_above, new_slack, new_rhs
        removed.append((alive, normal))
        alive = stay
    solved = {0: rhs[0] * inverse(slack[0])}
    for order, normal in reversed(removed):
        for n in range(1, len(order), 2):
            nb, na, ns, nr = normal[order[n]]
            item = nr + nb * solved[order[n - 1]]
            if na is not None:
                item = item + na * solved[order[n + 1]]
            solved[order[n]] = item
    for k in range(slabs):
        ends[k, pl.ds(0, 8), :] = solved[2 * k]
        ends[k, pl.ds(8, 8), :] = solved[2 * k + 1]


def last_kernel(ids, weather, scale_emit, ends, kept, cells, state, grad, lines):
    rows = sublane()
    low = rows < 4

    def table(s, column):
        return weather[ids[s], column]

    parts = []
    for f in range(2):
        factor = choose(rows % 4, [table(s, 6 + f) for s in range(4)])
        for yb in range(4):
            v = f * 4 + yb
            total = None
            for zp in range(4):
                j = v * 4 + zp
                weight = factor * choose(rows // 4, [scale_emit[2 * zp], scale_emit[2 * zp + 1]])
                first = ends[j, pl.ds(0, 8), :]
                last = ends[j, pl.ds(8, 8), :]
                a1, b1, c1, a2, b2, c2 = (kept[j, pl.ds(n * 8, 8), :] for n in range(6))
                two = a2 + b2 * first + c2 * last
                one = a1 + b1 * first + c1 * two
                for x, item in enumerate((first, one, two, last)):
                    lines[pl.ds(v * 128 + zp * 32 + x, 8, stride=4), :] = item
                item = weight * ((first + one) + (two + last))
                total = item if total is None else total + item
            parts.append(jnp.sum(total, axis=0, keepdims=True))
        for z in range(8):
            for sp in range(2):
                for h in range(2):
                    base = (f * 4 + 2 * h) * 128 + z * 16 + sp * 8
                    even, odd = pair_halves(
                        lines[pl.ds(base, 8), :], lines[pl.ds(base + 128, 8), :], low
                    )
                    for s, item in ((2 * sp, even), (2 * sp + 1, odd)):
                        state[pl.ds(s * 256 + f * 128 + z * 16 + h * 8, 8), :] = item
    width = 512
    start = jnp.min(cells[...] % width, axis=1, keepdims=True)
    place = lax.broadcasted_iota(jnp.int32, (128, width), 1)
    window = jnp.where((place >= start) & (place < start + 4), 1.0, 0.0).astype(jnp.bfloat16)
    sums = [jnp.concatenate(parts[f * 4 : f * 4 + 4], axis=1) for f in range(2)]
    sums = jnp.concatenate(sums + [jnp.zeros((6, width), F32)], axis=0)
    picked = jnp.zeros((8, 128), F32)
    for _ in range(3):
        piece = sums.astype(jnp.bfloat16)
        sums = sums - piece.astype(F32)
        picked = picked + lax.dot_general(
            piece, window, (((1,), (1,)), ((), ())), preferred_element_type=F32
        )
    grad[...] = picked[0:2, :]


def rows_of(block):
    s, f, z, x, y = block.shape
    return block.reshape(s, f, z, x, y // 128, 128).transpose(0, 1, 2, 4, 3, 5).reshape(-1, 128)


def on_device(
    cotangent, scenario_ids, weather, landuse, class_diff, level_scale, emit_profile, building_cells
):
    smem = pl.BlockSpec(memory_space=pltpu.SMEM)
    vmem = pl.BlockSpec(memory_space=pltpu.VMEM)
    params = pltpu.CompilerParams(vmem_limit_bytes=32 * 1024 * 1024)
    slabs = lax.axis_size("tile")
    cot = rows_of(cotangent)
    classes = landuse.reshape(4, 4, 128).transpose(1, 0, 2).reshape(16, 128)
    sent, kept = pl.pallas_call(
        first_kernel,
        out_shape=(
            jax.ShapeDtypeStruct((slabs, SEND, 128), F32),
            jax.ShapeDtypeStruct((slabs, 48, 128), F32),
        ),
        in_specs=[smem] * 4 + [vmem] * 2,
        out_specs=(vmem, vmem),
        scratch_shapes=[pltpu.VMEM((1024, 128), F32)] * 6 + [pltpu.VMEM((32, 128), F32)],
        compiler_params=params,
    )(scenario_ids, weather, class_diff, level_scale, cot, classes)
    got = lax.all_to_all(sent, "tile", 0, 0)
    place = lax.axis_index("tile").astype(jnp.int32).reshape(1)
    ends = pl.pallas_call(
        middle_kernel,
        out_shape=jax.ShapeDtypeStruct((slabs, 16, 128), F32),
        in_specs=[smem] * 4 + [vmem],
        out_specs=vmem,
        compiler_params=params,
    )(place, scenario_ids, weather, level_scale, got)
    ends = lax.all_to_all(ends, "tile", 0, 0)
    state, grad = pl.pallas_call(
        last_kernel,
        out_shape=(
            jax.ShapeDtypeStruct((1024, 128), F32),
            jax.ShapeDtypeStruct((2, 128), F32),
        ),
        in_specs=[smem] * 3 + [vmem] * 3,
        out_specs=(vmem, vmem),
        scratch_shapes=[pltpu.VMEM((1024, 128), F32)],
        compiler_params=params,
    )(scenario_ids, weather, emit_profile, ends, kept, building_cells)
    state = state.reshape(4, 2, 8, 4, 4, 128).transpose(0, 1, 2, 4, 3, 5).reshape(cotangent.shape)
    grad = grad + lax.ppermute(grad, "scen", [(i, i ^ 1) for i in range(8)])
    grad = grad + sum(
        lax.ppermute(grad, "scen", [(i, (i + step) % 8) for i in range(8)]) for step in (2, 4, 6)
    )
    return (state, grad)


def solution(mesh):
    placed = (
        P("scen", None, None, "tile", None),
        P("scen"),
        P(),
        P("tile", None),
        P(),
        P(),
        P(),
        P("tile", None),
    )
    return jax.shard_map(
        on_device,
        mesh=mesh,
        in_specs=placed,
        out_specs=(P("scen", None, None, "tile", None), P(None, "tile")),
        check_vma=False,
    )
```

time: 974 us -> 64.6 us (0.07)
  waiting for transfers between devices: 493 us -> 26.5 us
  local copies, waits for them, and re-layouts: 258 us -> 2.59 us
  other arithmetic: 175 us -> 0.57 us
  starting transfers between devices: 5.47 us -> 25.7 us
  blocking collectives: 15.6 us -> 0 us
  between operations: 14.6 us -> 0.71 us
    all_gather x6 -> x0, waiting for transfers between devices: 490 us -> none  [the longest x1 82.2 us: on_device(): lax.all_gather(local_value[:, :, :, 0:1], 'tile', axis=3, tiled=True)]
    slice x164 -> x0, local copies, waits for them, and re-layouts: 154 us -> none  [the longest x64 67.8 us: forward_block(): denom = mid[row] - low[row] * ratio_prev]
    dynamic_update_slice x64 -> x0, other arithmetic: 128 us -> none  [on_device(): lax.scan(forward_step, (zeros_plane, zeros_plane), (value_first, value_la...]
    another operation x109 -> x0, local copies, waits for them, and re-layouts: 30.9 us -> none
    all_to_all x0 -> x2, waiting for transfers between devices: none -> 24.1 us  [the longest x1 13.8 us: on_device(): got = lax.all_to_all(sent, 'tile', 0, 0)]
    dynamic_update_slice x64 -> x0, local copies, waits for them, and re-layouts: 19.9 us -> none  [blocked_solve(): lax.scan(forward_block, (zeros_rest, zeros_rest), (grouped(lower), groupe...]
    all_to_all x0 -> x2, starting transfers between devices: none -> 17 us  [the longest x1 11.9 us: on_device(): got = lax.all_to_all(sent, 'tile', 0, 0)]
    psum x1 -> x0, blocking collectives: 15.6 us -> none  [on_device(): control_grad = lax.psum(partial_grad, 'scen')]
  transfers between devices with their start and end apart: 8 -> 6, of which waited for: 6 -> 5; matrix products, arithmetic and copies ran while one was open for 1% -> 0% of each run, Pallas kernels for 0% -> 0%
where the time goes in v1:
time: 64.6 us; the launch traced here: 64.2 us
  waiting for transfers between devices  26.5 us (41%)
  starting transfers between devices  25.7 us (40%)
  Pallas kernels  8.1 us (13%)
  local copies, waits for them, and re-layouts  2.59 us (4%)
  between operations  0.71 us (1%)
    all_to_all x1, waiting for transfers between devices, on_device(): got = lax.all_to_all(sent, 'tile', 0, 0)  13.8 us
    all_to_all x1, starting transfers between devices, on_device(): got = lax.all_to_all(sent, 'tile', 0, 0)  11.9 us
    all_to_all x1, waiting for transfers between devices, on_device(): ends = lax.all_to_all(ends, 'tile', 0, 0)  10.3 us
    all_to_all x1, starting transfers between devices, on_device(): ends = lax.all_to_all(ends, 'tile', 0, 0)  5.13 us
    ppermute x3, starting transfers between devices, on_device(): lax.ppermute(grad, 'scen', [(i, (i + step) % 8) for i in range(8)])  4.99 us
    ppermute x1, starting transfers between devices, on_device(): grad = grad + lax.ppermute(grad, 'scen', [(i, i ^ 1) for i in range(8)])  3.76 us
    pallas_call x1, Pallas kernels, on_device(): pl.pallas_call(first_kernel, out_shape=(jax.ShapeDtypeStruct((slabs, SEND...  3.56 us
    unnamed x16, local copies, waits for them, and re-layouts  2.59 us
  transfers between devices with their start and end apart: 6, of which 5 were waited for; matrix products, arithmetic and copies ran while one was open for 0% of the time, Pallas kernels for 0%

profile of v1, /device:TPU:1, one launch (start us, length us, event | category | flops | bytes accessed | tf_op | source)
XLA Modules:
  0.0 64.2 jit_solution(18303821871560463517)
XLA Ops:
  0.6 0.8 %copy.14.weather = f32[64,8]{1,0:T(8,128)S(1)} copy(f32[64,8]{0,1:T(8,128)} %param.10) | data formatting | bytes 4096 | tf_op args[2]
  1.4 0.0 copy-start.3
  1.5 0.6 %copy-done.4 = f32[2,17]{1,0:T(2,128)S(1)} copy-done((f32[2,17]{1,0:T(2,128)S(1)}, f32[2,17]{1,0:T(2,128)}, u32[]{:S(2)}) %copy-start.4) | copy-done | bytes 160
  2.1 0.0 copy-done.2
  2.1 0.0 copy-done.3
  2.1 1.0 %copy-done = f32[4,2,8,4,512]{4,3,2,1,0:T(4,128)S(1)} copy-done((f32[4,2,8,4,512]{4,3,2,1,0:T(4,128)S(1)}, f32[4,2,8,4,512]{4,3,2,1,0:T(4,128)}, u32[]{:S(2)}) %copy-start) | copy-done | bytes 524312
  3.1 3.6 %shard_map.95 = (f32[32,24,128]{2,1,0:T(8,128)}, f32[32,48,128]{2,1,0:T(8,128)S(1)}) custom-call(s32[4]{0:T(128)S(1)} %copy-done.2, f32[64,8]{1,0:T(8,128)S(1)} %copy.14.weather, f32[2,17]{1,0:T(2,128)S(1)} %copy-done.4, f32[8]{0:T(128)S(1)} %copy-done.3, f32[1024,128]{1,0:T(8,128)S(1)} %bitcast.16, s32[16,128]{1,0:T(8,128)S(1)} %bitcast.17), custom_call_target="tpu_custom_call" | custom-call | tf_op jit(solution)/shard_map/pallas_call | solution.py:481
  6.7 11.9 %all-to-all-start = ((f32[32,24,128]{2,1,0:T(8,128)}), f32[32,24,128]{2,1,0:T(8,128)S(1)}, u32[]{:S(2)}, u32[]{:S(2)}) async-start(f32[32,24,128]{2,1,0:T(8,128)} %get-tuple-element.6), calls=%async_computation | async-start | bytes 786432 | tf_op jit(solution)/shard_map/all_to_all | solution.py:492
  18.6 13.8 %all-to-all-done.got = f32[32,24,128]{2,1,0:T(8,128)S(1)} async-done(((f32[32,24,128]{2,1,0:T(8,128)}), f32[32,24,128]{2,1,0:T(8,128)S(1)}, u32[]{:S(2)}, u32[]{:S(2)}) %all-to-all-start) | async-done | bytes 393248 | tf_op jit(solution)/shard_map/all_to_all | solution.py:492
  32.4 2.3 %shard_map.96 = f32[32,16,128]{2,1,0:T(8,128)} custom-call(s32[1]{0:T(128)} %bitcast.place, s32[4]{0:T(128)S(1)} %copy-done.2, f32[64,8]{1,0:T(8,128)S(1)} %copy.14.weather, f32[8]{0:T(128)S(1)} %copy-done.3, f32[32,24,128]{2,1,0:T(8,128)S(1)} %all-to-all-done.got), custom_call_target="tpu_custom_call" | custom-call | tf_op jit(solution)/shard_map/pallas_call | solution.py:494
  34.7 5.1 %all-to-all-start.1 = ((f32[32,16,128]{2,1,0:T(8,128)}), f32[32,16,128]{2,1,0:T(8,128)S(1)}, u32[]{:S(2)}, u32[]{:S(2)}) async-start(f32[32,16,128]{2,1,0:T(8,128)} %shard_map.96), calls=%async_computation.1 | async-start | bytes 524288 | tf_op jit(solution)/shard_map/all_to_all | solution.py:501
  39.9 0.1 copy.15.cells
  40.0 10.3 %all-to-all-done.1.ends = f32[32,16,128]{2,1,0:T(8,128)S(1)} async-done(((f32[32,16,128]{2,1,0:T(8,128)}), f32[32,16,128]{2,1,0:T(8,128)S(1)}, u32[]{:S(2)}, u32[]{:S(2)}) %all-to-all-start.1) | async-done | bytes 262176 | tf_op jit(solution)/shard_map/all_to_all | solution.py:501
  50.3 0.0 copy-done.5
  50.3 2.2 %shard_map.97 = (f32[1024,128]{1,0:T(8,128)}, f32[2,128]{1,0:T(2,128)S(1)}) custom-call(s32[4]{0:T(128)S(1)} %copy-done.2, f32[64,8]{1,0:T(8,128)S(1)} %copy.14.weather, f32[8]{0:T(128)S(1)} %copy-done.5, f32[32,16,128]{2,1,0:T(8,128)S(1)} %all-to-all-done.1.ends, f32[32,48,128]{2,1,0:T(8,128)S(1)} %get-tuple-element.7.kept, s32[128,16]{1,0:T(8,128)S(1)} %copy.15.cells), custom_call_target="tpu_custom_call" | custom-call | tf_op jit(solution)/shard_map/pallas_call | solution.py:502
  52.5 3.8 %collective-permute-start = (f32[2,128]{1,0:T(2,128)S(1)}, f32[2,128]{1,0:T(2,128)S(1)}, u32[]{:S(2)}, u32[]{:S(2)}) collective-permute-start(f32[2,128]{1,0:T(2,128)S(1)} %get-tuple-element.9), channel_id=1, source_target_pairs={{0,32},{32,0},{64,96},{96,64},{128,160},{160,128},{192,224},{224,1... | collective-permute-start | bytes 3080 | tf_op jit(solution)/shard_map/ppermute | solution.py:514
  56.2 0.8 %collective-permute-done = f32[2,128]{1,0:T(2,128)S(1)} collective-permute-done((f32[2,128]{1,0:T(2,128)S(1)}, f32[2,128]{1,0:T(2,128)S(1)}, u32[]{:S(2)}, u32[]{:S(2)}) %collective-permute-start) | collective-permute-done | bytes 1056 | tf_op jit(solution)/shard_map/ppermute | solution.py:514
  57.1 1.3 %collective-permute-start.1 = (f32[2,128]{1,0:T(2,128)S(1)}, f32[2,128]{1,0:T(2,128)S(1)}, u32[]{:S(2)}, u32[]{:S(2)}) collective-permute-start(f32[2,128]{1,0:T(2,128)S(1)} %add.12), channel_id=1, source_target_pairs={{0,64},{32,96},{64,128},{96,160},{128,192},{160,224},{192,0},{224,... | collective-permute-start | bytes 3080 | tf_op jit(solution)/shard_map/ppermute | solution.py:516
  58.4 2.6 %collective-permute-start.2 = (f32[2,128]{1,0:T(2,128)S(1)}, f32[2,128]{1,0:T(2,128)S(1)}, u32[]{:S(2)}, u32[]{:S(2)}) collective-permute-start(f32[2,128]{1,0:T(2,128)S(1)} %add.12), channel_id=1, source_target_pairs={{0,128},{32,160},{64,192},{96,224},{128,0},{160,32},{192,64},{224,... | collective-permute-start | bytes 3080 | tf_op jit(solution)/shard_map/ppermute | solution.py:516
  61.0 1.1 %collective-permute-start.3 = (f32[2,128]{1,0:T(2,128)S(1)}, f32[2,128]{1,0:T(2,128)S(1)}, u32[]{:S(2)}, u32[]{:S(2)}) collective-permute-start(f32[2,128]{1,0:T(2,128)S(1)} %add.12), channel_id=1, source_target_pairs={{0,192},{32,224},{64,0},{96,32},{128,64},{160,96},{192,128},{224,1... | collective-permute-start | bytes 3080 | tf_op jit(solution)/shard_map/ppermute | solution.py:516
  62.0 0.0 collective-permute-done.1
  62.0 0.2 collective-permute-done.2
  62.3 1.4 %collective-permute-done.3 = f32[2,128]{1,0:T(2,128)S(1)} collective-permute-done((f32[2,128]{1,0:T(2,128)S(1)}, f32[2,128]{1,0:T(2,128)S(1)}, u32[]{:S(2)}, u32[]{:S(2)}) %collective-permute-start.3) | collective-permute-done | bytes 1056 | tf_op jit(solution)/shard_map/ppermute | solution.py:516
  63.6 0.6 add_add_fusion
  (9 shorter events, 0.0 us)
Async XLA Ops:
  0.6 0.8 %copy-start.1 = (s32[4,512]{1,0:T(4,128)S(1)}, s32[4,512]{1,0:T(4,128)}, u32[]{:S(2)}) copy-start(s32[4,512]{1,0:T(4,128)} %param.11) | copy-start | bytes 24580
  1.4 0.7 %copy-start.4 = (f32[2,17]{1,0:T(2,128)S(1)}, f32[2,17]{1,0:T(2,128)}, u32[]{:S(2)}) copy-start(f32[2,17]{1,0:T(2,128)} %class_diff.1) | copy-start | bytes 412
  1.4 0.7 %copy-start.2 = (s32[4]{0:T(128)S(1)}, s32[4]{0:T(128)}, u32[]{:S(2)}) copy-start(s32[4]{0:T(128)} %ids.5) | copy-start | bytes 52
  1.4 0.7 %copy-start.3 = (f32[8]{0:T(128)S(1)}, f32[8]{0:T(128)}, u32[]{:S(2)}) copy-start(f32[8]{0:T(128)} %scale.3) | copy-start | bytes 100
  2.1 1.0 %copy-start = (f32[4,2,8,4,512]{4,3,2,1,0:T(4,128)S(1)}, f32[4,2,8,4,512]{4,3,2,1,0:T(4,128)}, u32[]{:S(2)}) copy-start(f32[4,2,8,4,512]{4,3,2,1,0:T(4,128)} %param.8) | copy-start | bytes 1572868
  6.7 25.7 %all-to-all-start = ((f32[32,24,128]{2,1,0:T(8,128)}), f32[32,24,128]{2,1,0:T(8,128)S(1)}, u32[]{:S(2)}, u32[]{:S(2)}) async-start(f32[32,24,128]{2,1,0:T(8,128)} %get-tuple-element.6), calls=%async_computation | async-start | bytes 786432 | tf_op jit(solution)/shard_map/all_to_all | solution.py:492
  34.7 5.1 %copy-start.6 = (s32[128,16]{0,1:T(8,128)S(1)}, s32[128,16]{0,1:T(8,128)}, u32[]{:S(2)}) copy-start(s32[128,16]{0,1:T(8,128)} %param.15) | copy-start | bytes 24580
  34.7 15.5 %all-to-all-start.1 = ((f32[32,16,128]{2,1,0:T(8,128)}), f32[32,16,128]{2,1,0:T(8,128)S(1)}, u32[]{:S(2)}, u32[]{:S(2)}) async-start(f32[32,16,128]{2,1,0:T(8,128)} %shard_map.96), calls=%async_computation.1 | async-start | bytes 524288 | tf_op jit(solution)/shard_map/all_to_all | solution.py:501
  40.0 10.3 %copy-start.5 = (f32[8]{0:T(128)S(1)}, f32[8]{0:T(128)}, u32[]{:S(2)}) copy-start(f32[8]{0:T(128)} %scale_emit.1) | copy-start | bytes 100
  52.5 4.6 %collective-permute-start = (f32[2,128]{1,0:T(2,128)S(1)}, f32[2,128]{1,0:T(2,128)S(1)}, u32[]{:S(2)}, u32[]{:S(2)}) collective-permute-start(f32[2,128]{1,0:T(2,128)S(1)} %get-tuple-element.9), channel_id=1, source_target_pairs={{0,32},{32,0},{64,96},{96,64},{128,160},{160,128},{192,224},{224,1... | collective-permute-start | bytes 3080 | tf_op jit(solution)/shard_map/ppermute | solution.py:514
  57.1 5.0 %collective-permute-start.1 = (f32[2,128]{1,0:T(2,128)S(1)}, f32[2,128]{1,0:T(2,128)S(1)}, u32[]{:S(2)}, u32[]{:S(2)}) collective-permute-start(f32[2,128]{1,0:T(2,128)S(1)} %add.12), channel_id=1, source_target_pairs={{0,64},{32,96},{64,128},{96,160},{128,192},{160,224},{192,0},{224,... | collective-permute-start | bytes 3080 | tf_op jit(solution)/shard_map/ppermute | solution.py:516
  58.4 3.9 %collective-permute-start.2 = (f32[2,128]{1,0:T(2,128)S(1)}, f32[2,128]{1,0:T(2,128)S(1)}, u32[]{:S(2)}, u32[]{:S(2)}) collective-permute-start(f32[2,128]{1,0:T(2,128)S(1)} %add.12), channel_id=1, source_target_pairs={{0,128},{32,160},{64,192},{96,224},{128,0},{160,32},{192,64},{224,... | collective-permute-start | bytes 3080 | tf_op jit(solution)/shard_map/ppermute | solution.py:516
  61.0 2.7 %collective-permute-start.3 = (f32[2,128]{1,0:T(2,128)S(1)}, f32[2,128]{1,0:T(2,128)S(1)}, u32[]{:S(2)}, u32[]{:S(2)}) collective-permute-start(f32[2,128]{1,0:T(2,128)S(1)} %add.12), channel_id=1, source_target_pairs={{0,192},{32,224},{64,0},{96,32},{128,64},{160,96},{192,128},{224,1... | collective-permute-start | bytes 3080 | tf_op jit(solution)/shard_map/ppermute | solution.py:516

commit v2 on v1

--- a/solution.py
+++ b/solution.py
@@ -48,9 +48,10 @@
     )
 
 
-def solve_levels(cot, surf, scale, table, out, hold_a, hold_c, low):
+def solve_levels(cot, surf, scale, table, out, hold_a, hold_c, low, arrivals):
     half = [(scale[z] + scale[z + 1]) * 0.5 for z in range(7)]
     for pair in range(2):
+        arrivals[pair].wait()
         chains = [(s, f, h) for s in (2 * pair, 2 * pair + 1) for f in range(2) for h in range(2)]
         rated = [surf[f][h] * table(s, 2) for s, f, h in chains]
         winds = [table(s, 5) for s, f, h in chains]
@@ -239,15 +240,41 @@
 
 
 def first_kernel(
-    ids, weather, class_diff, scale, cot, landuse, sent, kept,
-    levels, turned, faces, hold_a, hold_b, hold_c, surf_rows,
+    ids_in, weather_in, class_diff_in, scale_in, emit_in, landuse_in, cells_in, cot_in,
+    sent, kept, vectors, window,
+    ids, weather, class_diff, scale, emit, landuse, cells, cot,
+    levels, turned, faces, hold_a, hold_b, hold_c, surf_rows, done,
 ):
+    small = [
+        pltpu.make_async_copy(source, target, done.at[n])
+        for n, (source, target) in enumerate(
+            (
+                (ids_in, ids),
+                (weather_in, weather),
+                (class_diff_in, class_diff),
+                (scale_in, scale),
+                (emit_in, emit),
+                (landuse_in, landuse),
+                (cells_in, cells),
+            )
+        )
+    ]
+    halves = [
+        pltpu.make_async_copy(
+            cot_in.at[pl.ds(n * 512, 512), :], cot.at[pl.ds(n * 512, 512), :], done.at[7 + n]
+        )
+        for n in range(2)
+    ]
+    for copy in small + halves:
+        copy.start()
+    for copy in small:
+        copy.wait()
     rows = sublane()
     lanes = lane()
     low = rows < 4
 
     def table(s, column):
-        return weather[ids[s], column]
+        return weather[column, ids[s]]
 
     classes = [landuse[pl.ds(0, 8), :], landuse[pl.ds(8, 8), :]]
     surf = [[surface(item, class_diff, f) for item in classes] for f in range(2)]
@@ -280,7 +307,38 @@
         start = jnp.broadcast_to(jnp.sum(start, axis=0, keepdims=True), (8, 128))
         leak.append(start * 0.5 * rate_y)
 
-    solve_levels(cot, surf, scale, table, levels, hold_a, hold_c, low)
+    rate_x = choose(rows % 4, [table(s, 0) for s in range(4)])
+    wind_x = choose(rows % 4, [table(s, 3) for s in range(4)])
+    vectors[0] = rate_x
+    vectors[1] = wind_x
+    for f in range(2):
+        factor = choose(rows % 4, [table(s, 6 + f) for s in range(4)])
+        for zp in range(4):
+            vectors[2 + f * 4 + zp] = factor * choose(rows // 4, [emit[2 * zp], emit[2 * zp + 1]])
+    scales = [choose(rows // 4, [scale[2 * zp], scale[2 * zp + 1]]) for zp in range(4)]
+    for v in range(8):
+        line = [surf_rows[pl.ds(v * 4 + x, 1), :] for x in range(4)]
+        steps = [(line[x] + line[x + 1]) * 0.5 for x in range(3)]
+        four = surf_rows[pl.ds((v // 2) * 8, 8), :]
+        four = four if v % 2 == 0 else swap_halves(four)
+        for zp in range(4):
+            j = v * 4 + zp
+            rate = rate_x * scales[zp]
+            one_inv, one_fill, one_upper, two_inv, two_fill, two_slack, two_next = inner_coefs(
+                *(rate * step for step in steps), wind_x
+            )
+            for n, item in enumerate(
+                (one_inv, one_fill, one_upper, two_inv, two_fill * two_inv, two_next * two_inv)
+            ):
+                kept[j, pl.ds(n * 8, 8), :] = item
+            tail = jnp.where(rows == 4, scale[2 * zp], scale[2 * zp + 1])
+            sent[j, pl.ds(16, 8), :] = jnp.where(low, four, tail)
+    width = window.shape[0]
+    start = jnp.min(cells[...] % width, axis=0, keepdims=True)
+    place = lax.broadcasted_iota(jnp.int32, (width, 128), 0)
+    window[...] = jnp.where((place >= start) & (place < start + 4), 1.0, 0.0).astype(jnp.bfloat16)
+
+    solve_levels(cot, surf, scale, table, levels, hold_a, hold_c, low, halves)
     for v in range(8):
         block = pl.ds(v * 128, 128)
         turned[block, :] = levels[block, :].T
@@ -289,41 +347,28 @@
         block = pl.ds(v * 128, 128)
         levels[block, :] = turned[block, :].T
 
-    rate_x = choose(rows % 4, [table(s, 0) for s in range(4)])
-    wind_x = choose(rows % 4, [table(s, 3) for s in range(4)])
     for v in range(8):
         line = [surf_rows[pl.ds(v * 4 + x, 1), :] for x in range(4)]
         steps = [(line[x] + line[x + 1]) * 0.5 for x in range(3)]
-        four = surf_rows[pl.ds((v // 2) * 8, 8), :]
         for zp in range(4):
             j = v * 4 + zp
-            rate = rate_x * choose(rows // 4, [scale[2 * zp], scale[2 * zp + 1]])
+            rate = rate_x * scales[zp]
             e01, e12, e23 = (rate * step for step in steps)
             rhs = [levels[pl.ds(v * 128 + zp * 32 + x, 8, stride=4), :] for x in range(4)]
-            one_inv, one_fill, one_upper, two_inv, two_fill, two_slack, two_next = inner_coefs(
-                e01, e12, e23, wind_x
-            )
-            one = rhs[1] * one_inv
-            two = (rhs[2] + e12 * one) * two_inv
+            one = rhs[1] * kept[j, pl.ds(0, 8), :]
+            two = (rhs[2] + e12 * one) * kept[j, pl.ds(24, 8), :]
+            one_upper = kept[j, pl.ds(16, 8), :]
             sent[j, pl.ds(0, 8), :] = rhs[0] + (e01 + wind_x) * (one + one_upper * two)
             sent[j, pl.ds(8, 8), :] = rhs[3] + e23 * two
-            sent[j, pl.ds(16, 8), :] = four if v % 2 == 0 else swap_halves(four)
-            for n, item in enumerate(
-                (one, one_fill, one_upper, two, two_fill * two_inv, two_next * two_inv)
-            ):
-                kept[j, pl.ds(n * 8, 8), :] = item
-
-
-def middle_kernel(place, ids, weather, scale, got, ends):
+            kept[j, pl.ds(0, 8), :] = one
+            kept[j, pl.ds(24, 8), :] = two
+
+
+def middle_kernel(vectors, got, ends):
     rows = sublane()
-
-    def table(s, column):
-        return weather[ids[s], column]
-
-    rate = choose(rows % 4, [table(s, 0) for s in range(4)])
-    wind = choose(rows % 4, [table(s, 3) for s in range(4)])
-    zp = place[0] % 4
-    rate = rate * choose(rows // 4, [scale[2 * zp], scale[2 * zp + 1]])
+    scale = jnp.where(rows < 4, got[0, pl.ds(20, 1), :], got[0, pl.ds(21, 1), :])
+    rate = vectors[0] * scale
+    wind = vectors[1]
     slabs = got.shape[0]
     below, above, slack, rhs = [], [], [], []
     line = None
@@ -413,32 +458,43 @@
         ends[k, pl.ds(8, 8), :] = solved[2 * k + 1]
 
 
-def last_kernel(ids, weather, scale_emit, ends, kept, cells, state, grad, lines):
-    rows = sublane()
-    low = rows < 4
-
-    def table(s, column):
-        return weather[ids[s], column]
-
+def inner_rows(ends, kept, j):
+    first = ends[j, pl.ds(0, 8), :]
+    last = ends[j, pl.ds(8, 8), :]
+    a1, b1, c1, a2, b2, c2 = (kept[j, pl.ds(n * 8, 8), :] for n in range(6))
+    two = a2 + b2 * first + c2 * last
+    one = a1 + b1 * first + c1 * two
+    return first, one, two, last
+
+
+def sums_kernel(vectors, window, ends, kept, grad):
     parts = []
+    for v in range(8):
+        total = None
+        for zp in range(4):
+            first, one, two, last = inner_rows(ends, kept, v * 4 + zp)
+            item = vectors[2 + (v // 4) * 4 + zp] * ((first + one) + (two + last))
+            total = item if total is None else total + item
+        parts.append(jnp.sum(total, axis=0, keepdims=True))
+    sums = [jnp.concatenate(parts[f * 4 : f * 4 + 4], axis=1) for f in range(2)]
+    pieces = []
+    for _ in range(3):
+        piece = [item.astype(jnp.bfloat16).astype(F32) for item in sums]
+        sums = [item - cut for item, cut in zip(sums, piece)]
+        pieces += piece
+    pieces = jnp.concatenate(pieces + [jnp.zeros((2, sums[0].shape[1]), F32)], axis=0)
+    picked = jnp.dot(pieces.astype(jnp.bfloat16), window[...], preferred_element_type=F32)
+    grad[...] = (picked[0:2, :] + picked[2:4, :]) + picked[4:6, :]
+
+
+def state_kernel(ends, kept, state, lines):
+    low = sublane() < 4
     for f in range(2):
-        factor = choose(rows % 4, [table(s, 6 + f) for s in range(4)])
         for yb in range(4):
             v = f * 4 + yb
-            total = None
             for zp in range(4):
-                j = v * 4 + zp
-                weight = factor * choose(rows // 4, [scale_emit[2 * zp], scale_emit[2 * zp + 1]])
-                first = ends[j, pl.ds(0, 8), :]
-                last = ends[j, pl.ds(8, 8), :]
-                a1, b1, c1, a2, b2, c2 = (kept[j, pl.ds(n * 8, 8), :] for n in range(6))
-                two = a2 + b2 * first + c2 * last
-                one = a1 + b1 * first + c1 * two
-                for x, item in enumerate((first, one, two, last)):
+                for x, item in enumerate(inner_rows(ends, kept, v * 4 + zp)):
                     lines[pl.ds(v * 128 + zp * 32 + x, 8, stride=4), :] = item
-                item = weight * ((first + one) + (two + last))
-                total = item if total is None else total + item
-            parts.append(jnp.sum(total, axis=0, keepdims=True))
         for z in range(8):
             for sp in range(2):
                 for h in range(2):
@@ -448,20 +504,6 @@
                     )
                     for s, item in ((2 * sp, even), (2 * sp + 1, odd)):
                         state[pl.ds(s * 256 + f * 128 + z * 16 + h * 8, 8), :] = item
-    width = 512
-    start = jnp.min(cells[...] % width, axis=1, keepdims=True)
-    place = lax.broadcasted_iota(jnp.int32, (128, width), 1)
-    window = jnp.where((place >= start) & (place < start + 4), 1.0, 0.0).astype(jnp.bfloat16)
-    sums = [jnp.concatenate(parts[f * 4 : f * 4 + 4], axis=1) for f in range(2)]
-    sums = jnp.concatenate(sums + [jnp.zeros((6, width), F32)], axis=0)
-    picked = jnp.zeros((8, 128), F32)
-    for _ in range(3):
-        piece = sums.astype(jnp.bfloat16)
-        sums = sums - piece.astype(F32)
-        picked = picked + lax.dot_general(
-            piece, window, (((1,), (1,)), ((), ())), preferred_element_type=F32
-        )
-    grad[...] = picked[0:2, :]
 
 
 def rows_of(block):
@@ -472,49 +514,62 @@
 def on_device(
     cotangent, scenario_ids, weather, landuse, class_diff, level_scale, emit_profile, building_cells
 ):
-    smem = pl.BlockSpec(memory_space=pltpu.SMEM)
+    hbm = pl.BlockSpec(memory_space=pltpu.HBM)
     vmem = pl.BlockSpec(memory_space=pltpu.VMEM)
     params = pltpu.CompilerParams(vmem_limit_bytes=32 * 1024 * 1024)
     slabs = lax.axis_size("tile")
-    cot = rows_of(cotangent)
+    groups = lax.axis_size("scen")
+    width = cotangent.shape[4]
+    cells = building_cells.T
     classes = landuse.reshape(4, 4, 128).transpose(1, 0, 2).reshape(16, 128)
-    sent, kept = pl.pallas_call(
+    small = (scenario_ids, weather.T, class_diff, level_scale, emit_profile)
+    operands = (*small, classes, cells, rows_of(cotangent))
+    sent, kept, vectors, window = pl.pallas_call(
         first_kernel,
         out_shape=(
             jax.ShapeDtypeStruct((slabs, SEND, 128), F32),
             jax.ShapeDtypeStruct((slabs, 48, 128), F32),
+            jax.ShapeDtypeStruct((10, 8, 128), F32),
+            jax.ShapeDtypeStruct((width, cells.shape[1]), jnp.bfloat16),
         ),
-        in_specs=[smem] * 4 + [vmem] * 2,
-        out_specs=(vmem, vmem),
-        scratch_shapes=[pltpu.VMEM((1024, 128), F32)] * 6 + [pltpu.VMEM((32, 128), F32)],
+        in_specs=[hbm] * 8,
+        out_specs=(vmem,) * 4,
+        scratch_shapes=[pltpu.SMEM(item.shape, item.dtype) for item in small]
+        + [pltpu.VMEM(item.shape, item.dtype) for item in (classes, cells)]
+        + [pltpu.VMEM((1024, 128), F32)] * 7
+        + [pltpu.VMEM((32, 128), F32), pltpu.SemaphoreType.DMA((9,))],
         compiler_params=params,
-    )(scenario_ids, weather, class_diff, level_scale, cot, classes)
+    )(*(pltpu.with_memory_space_constraint(item, pltpu.HBM) for item in operands))
     got = lax.all_to_all(sent, "tile", 0, 0)
-    place = lax.axis_index("tile").astype(jnp.int32).reshape(1)
     ends = pl.pallas_call(
         middle_kernel,
         out_shape=jax.ShapeDtypeStruct((slabs, 16, 128), F32),
-        in_specs=[smem] * 4 + [vmem],
+        in_specs=[vmem] * 2,
         out_specs=vmem,
         compiler_params=params,
-    )(place, scenario_ids, weather, level_scale, got)
+    )(vectors, got)
     ends = lax.all_to_all(ends, "tile", 0, 0)
-    state, grad = pl.pallas_call(
-        last_kernel,
-        out_shape=(
-            jax.ShapeDtypeStruct((1024, 128), F32),
-            jax.ShapeDtypeStruct((2, 128), F32),
-        ),
-        in_specs=[smem] * 3 + [vmem] * 3,
-        out_specs=(vmem, vmem),
+    grad = pl.pallas_call(
+        sums_kernel,
+        out_shape=jax.ShapeDtypeStruct((2, cells.shape[1]), F32),
+        in_specs=[vmem] * 4,
+        out_specs=vmem,
+        compiler_params=params,
+    )(vectors, window, ends, kept)
+    state = pl.pallas_call(
+        state_kernel,
+        out_shape=jax.ShapeDtypeStruct((1024, 128), F32),
+        in_specs=[vmem] * 2,
+        out_specs=vmem,
         scratch_shapes=[pltpu.VMEM((1024, 128), F32)],
         compiler_params=params,
-    )(scenario_ids, weather, emit_profile, ends, kept, building_cells)
+    )(ends, kept)
+    grad = grad + lax.ppermute(grad, "scen", [(i, i ^ 1) for i in range(groups)])
+    grad = grad + sum(
+        lax.ppermute(grad, "scen", [(i, (i + step) % groups) for i in range(groups)])
+        for step in (2, 6, 4)
+    )
     state = state.reshape(4, 2, 8, 4, 4, 128).transpose(0, 1, 2, 4, 3, 5).reshape(cotangent.shape)
-    grad = grad + lax.ppermute(grad, "scen", [(i, i ^ 1) for i in range(8)])
-    grad = grad + sum(
-        lax.ppermute(grad, "scen", [(i, (i + step) % 8) for i in range(8)]) for step in (2, 4, 6)
-    )
     return (state, grad)
 
 

time: 64.6 us -> 57.8 us (0.89)
  blocking collectives: 0 us -> 40.7 us
  waiting for transfers between devices: 26.5 us -> 2.85 us
  starting transfers between devices: 25.7 us -> 8.14 us
  Pallas kernels: 8.1 us -> 4.75 us
  local copies, waits for them, and re-layouts: 2.59 us -> 0 us
    all_to_all x0 -> x2, blocking collectives: none -> 40.7 us  [the longest x1 25.5 us: on_device(): got = lax.all_to_all(sent, 'tile', 0, 0)]
    all_to_all x2 -> x0, waiting for transfers between devices: 24.1 us -> none  [the longest x1 13.8 us: on_device(): got = lax.all_to_all(sent, 'tile', 0, 0)]
    all_to_all x2 -> x0, starting transfers between devices: 17 us -> none  [the longest x1 11.9 us: on_device(): got = lax.all_to_all(sent, 'tile', 0, 0)]
    unnamed x16 -> x0, local copies, waits for them, and re-layouts: 2.59 us -> none
    pallas_call x1, Pallas kernels: 2.32 us -> 0.55 us  [on_device(): pl.pallas_call(middle_kernel, out_shape=jax.ShapeDtypeStruct((slabs, 16,...]
    pallas_call x1 -> x2, Pallas kernels: 2.21 us -> 1.14 us  [the longest x1 0.91 us: on_device(): pl.pallas_call(state_kernel, out_shape=jax.ShapeDtypeStruct((1024, 128),...]
  transfers between devices with their start and end apart: 6 -> 4, of which waited for: 5 -> 2; matrix products, arithmetic and copies ran while one was open for 0% -> 0% of each run, Pallas kernels for 0% -> 2%
where the time goes in v2:
time: 57.8 us; the launch traced here: 57.6 us
  blocking collectives  40.7 us (70%)
  starting transfers between devices  8.14 us (14%)
  Pallas kernels  4.75 us (8%)
  waiting for transfers between devices  2.85 us (5%)
  between operations  0.66 us (1%)
    all_to_all x1, blocking collectives, on_device(): got = lax.all_to_all(sent, 'tile', 0, 0)  25.5 us
    all_to_all x1, blocking collectives, on_device(): ends = lax.all_to_all(ends, 'tile', 0, 0)  15.2 us
    ppermute x3, starting transfers between devices, on_device(): lax.ppermute(grad, 'scen', [(i, (i + step) % groups) for i in range(group...  4.38 us
    ppermute x1, starting transfers between devices, on_device(): lax.ppermute(grad, 'scen', [(i, i ^ 1) for i in range(groups)])  3.76 us
    pallas_call x1, Pallas kernels, on_device(): pl.pallas_call(first_kernel, out_shape=(jax.ShapeDtypeStruct((slabs, SEND...  3.07 us
    ppermute x3, waiting for transfers between devices, on_device(): lax.ppermute(grad, 'scen', [(i, (i + step) % groups) for i in range(group...  2.03 us
  transfers between devices with their start and end apart: 4, of which 2 were waited for; matrix products, arithmetic and copies ran while one was open for 0% of the time, Pallas kernels for 2%

profile of v2, /device:TPU:1, one launch (start us, length us, event | category | flops | bytes accessed | tf_op | source)
XLA Modules:
  0.0 57.6 jit_solution(3476981029657716199)
XLA Ops:
  0.6 3.1 %shard_map.95 = (f32[32,24,128]{2,1,0:T(8,128)S(1)}, f32[32,48,128]{2,1,0:T(8,128)S(1)}, f32[10,8,128]{2,1,0:T(8,128)S(1)}, bf16[512,128]{1,0:T(8,128)(2,1)S(1)}) custom-call(s32[4]{0:T(128)} %ids_in.1, f32[8,64]{1,0:T(8,128)} %bitcast.21, f32[2,17]{1,0:T(2,128)} %class_diff_in.1, f32[8]{0:T(128)} %scale_in.1, f32[8]{0:T(128)} %emit_in.1, ...), custom_call_target="tpu_custom_call" | custom-call | tf_op jit(solution)/shard_map/pallas_call | solution.py:527
  3.7 25.5 %all_to_all.10.got = f32[32,24,128]{2,1,0:T(8,128)S(1)} all-to-all(f32[32,24,128]{2,1,0:T(8,128)S(1)} %get-tuple-element.7), channel_id=1, replica_groups=mesh['scen'=8,'tile'=32] {'tile'}, dimensions={0} | all-to-all | bytes 786432 | tf_op jit(solution)/shard_map/all_to_all | solution.py:543
  29.2 0.5 shard_map.96
  29.7 15.2 %all_to_all.11.ends = f32[32,16,128]{2,1,0:T(8,128)S(1)} all-to-all(f32[32,16,128]{2,1,0:T(8,128)S(1)} %shard_map.96), channel_id=1, replica_groups=mesh['scen'=8,'tile'=32] {'tile'}, dimensions={0} | all-to-all | bytes 524288 | tf_op jit(solution)/shard_map/all_to_all | solution.py:551
  44.9 0.2 shard_map.98
  45.2 3.8 %collective-permute-start = (f32[2,128]{1,0:T(2,128)S(1)}, f32[2,128]{1,0:T(2,128)S(1)}, u32[]{:S(2)}, u32[]{:S(2)}) collective-permute-start(f32[2,128]{1,0:T(2,128)S(1)} %shard_map.98), channel_id=1, source_target_pairs={{0,32},{32,0},{64,96},{96,64},{128,160},{160,128},{192,224},{224,1... | collective-permute-start | bytes 3080 | tf_op jit(solution)/shard_map/ppermute | solution.py:567
  48.9 0.8 %collective-permute-done = f32[2,128]{1,0:T(2,128)S(1)} collective-permute-done((f32[2,128]{1,0:T(2,128)S(1)}, f32[2,128]{1,0:T(2,128)S(1)}, u32[]{:S(2)}, u32[]{:S(2)}) %collective-permute-start) | collective-permute-done | bytes 1056 | tf_op jit(solution)/shard_map/ppermute | solution.py:567
  49.8 2.9 %collective-permute-start.3 = (f32[2,128]{1,0:T(2,128)S(1)}, f32[2,128]{1,0:T(2,128)S(1)}, u32[]{:S(2)}, u32[]{:S(2)}) collective-permute-start(f32[2,128]{1,0:T(2,128)S(1)} %add.12), channel_id=1, source_target_pairs={{0,128},{32,160},{64,192},{96,224},{128,0},{160,32},{192,64},{224,... | collective-permute-start | bytes 3080 | tf_op jit(solution)/shard_map/ppermute | solution.py:569
  52.7 0.8 %collective-permute-start.2 = (f32[2,128]{1,0:T(2,128)S(1)}, f32[2,128]{1,0:T(2,128)S(1)}, u32[]{:S(2)}, u32[]{:S(2)}) collective-permute-start(f32[2,128]{1,0:T(2,128)S(1)} %add.12), channel_id=1, source_target_pairs={{0,192},{32,224},{64,0},{96,32},{128,64},{160,96},{192,128},{224,1... | collective-permute-start | bytes 3080 | tf_op jit(solution)/shard_map/ppermute | solution.py:569
  53.4 0.7 %collective-permute-start.1 = (f32[2,128]{1,0:T(2,128)S(1)}, f32[2,128]{1,0:T(2,128)S(1)}, u32[]{:S(2)}, u32[]{:S(2)}) collective-permute-start(f32[2,128]{1,0:T(2,128)S(1)} %add.12), channel_id=1, source_target_pairs={{0,64},{32,96},{64,128},{96,160},{128,192},{160,224},{192,0},{224,... | collective-permute-start | bytes 3080 | tf_op jit(solution)/shard_map/ppermute | solution.py:569
  54.1 0.9 %shard_map.97 = f32[1024,128]{1,0:T(8,128)} custom-call(f32[32,16,128]{2,1,0:T(8,128)S(1)} %all_to_all.11.ends, f32[32,48,128]{2,1,0:T(8,128)S(1)} %get-tuple-element.8.kept), custom_call_target="tpu_custom_call" | custom-call | tf_op jit(solution)/shard_map/pallas_call | solution.py:559
  55.0 0.0 collective-permute-done.3
  55.0 0.0 collective-permute-done.2
  55.1 2.0 %collective-permute-done.1 = f32[2,128]{1,0:T(2,128)S(1)} collective-permute-done((f32[2,128]{1,0:T(2,128)S(1)}, f32[2,128]{1,0:T(2,128)S(1)}, u32[]{:S(2)}, u32[]{:S(2)}) %collective-permute-start.1) | collective-permute-done | bytes 1056 | tf_op jit(solution)/shard_map/ppermute | solution.py:569
  57.1 0.6 add_add_fusion
  (1 shorter events, 0.0 us)
Async XLA Ops:
  45.2 4.6 %collective-permute-start = (f32[2,128]{1,0:T(2,128)S(1)}, f32[2,128]{1,0:T(2,128)S(1)}, u32[]{:S(2)}, u32[]{:S(2)}) collective-permute-start(f32[2,128]{1,0:T(2,128)S(1)} %shard_map.98), channel_id=1, source_target_pairs={{0,32},{32,0},{64,96},{96,64},{128,160},{160,128},{192,224},{224,1... | collective-permute-start | bytes 3080 | tf_op jit(solution)/shard_map/ppermute | solution.py:567
  49.8 5.3 %collective-permute-start.3 = (f32[2,128]{1,0:T(2,128)S(1)}, f32[2,128]{1,0:T(2,128)S(1)}, u32[]{:S(2)}, u32[]{:S(2)}) collective-permute-start(f32[2,128]{1,0:T(2,128)S(1)} %add.12), channel_id=1, source_target_pairs={{0,128},{32,160},{64,192},{96,224},{128,0},{160,32},{192,64},{224,... | collective-permute-start | bytes 3080 | tf_op jit(solution)/shard_map/ppermute | solution.py:569
  52.7 2.4 %collective-permute-start.2 = (f32[2,128]{1,0:T(2,128)S(1)}, f32[2,128]{1,0:T(2,128)S(1)}, u32[]{:S(2)}, u32[]{:S(2)}) collective-permute-start(f32[2,128]{1,0:T(2,128)S(1)} %add.12), channel_id=1, source_target_pairs={{0,192},{32,224},{64,0},{96,32},{128,64},{160,96},{192,128},{224,1... | collective-permute-start | bytes 3080 | tf_op jit(solution)/shard_map/ppermute | solution.py:569
  53.4 3.6 %collective-permute-start.1 = (f32[2,128]{1,0:T(2,128)S(1)}, f32[2,128]{1,0:T(2,128)S(1)}, u32[]{:S(2)}, u32[]{:S(2)}) collective-permute-start(f32[2,128]{1,0:T(2,128)S(1)} %add.12), channel_id=1, source_target_pairs={{0,64},{32,96},{64,128},{96,160},{128,192},{160,224},{192,0},{224,... | collective-permute-start | bytes 3080 | tf_op jit(solution)/shard_map/ppermute | solution.py:569

commit v3 on v2

--- a/solution.py
+++ b/solution.py
@@ -6,7 +6,7 @@
 from jax.sharding import PartitionSpec as P
 
 F32 = jnp.float32
-SEND = 24
+SEND = 17
 
 
 def inverse(value):
@@ -46,6 +46,20 @@
         jnp.where(low, first, swap_halves(second)),
         jnp.where(low, swap_halves(first), second),
     )
+
+
+def exchange(items, lanes):
+    for bit in range(3):
+        step = 1 << bit
+        clear = (lanes // 16) // step % 2 == 0
+        out = list(items)
+        for n in range(8):
+            if n & step == 0:
+                first, second = items[n], items[n + step]
+                out[n] = jnp.where(clear, first, pltpu.roll(second, 16 * step, axis=1))
+                out[n + step] = jnp.where(clear, pltpu.roll(first, 128 - 16 * step, axis=1), second)
+        items = out
+    return items
 
 
 def solve_levels(cot, surf, scale, table, out, hold_a, hold_c, low, arrivals):
@@ -309,18 +323,16 @@
 
     rate_x = choose(rows % 4, [table(s, 0) for s in range(4)])
     wind_x = choose(rows % 4, [table(s, 3) for s in range(4)])
-    vectors[0] = rate_x
+    scales = [choose(rows // 4, [scale[2 * zp], scale[2 * zp + 1]]) for zp in range(4)]
+    vectors[0] = rate_x * choose(lanes // 16 % 4, scales)
     vectors[1] = wind_x
     for f in range(2):
         factor = choose(rows % 4, [table(s, 6 + f) for s in range(4)])
         for zp in range(4):
             vectors[2 + f * 4 + zp] = factor * choose(rows // 4, [emit[2 * zp], emit[2 * zp + 1]])
-    scales = [choose(rows // 4, [scale[2 * zp], scale[2 * zp + 1]]) for zp in range(4)]
     for v in range(8):
         line = [surf_rows[pl.ds(v * 4 + x, 1), :] for x in range(4)]
         steps = [(line[x] + line[x + 1]) * 0.5 for x in range(3)]
-        four = surf_rows[pl.ds((v // 2) * 8, 8), :]
-        four = four if v % 2 == 0 else swap_halves(four)
         for zp in range(4):
             j = v * 4 + zp
             rate = rate_x * scales[zp]
@@ -331,8 +343,10 @@
                 (one_inv, one_fill, one_upper, two_inv, two_fill * two_inv, two_next * two_inv)
             ):
                 kept[j, pl.ds(n * 8, 8), :] = item
-            tail = jnp.where(rows == 4, scale[2 * zp], scale[2 * zp + 1])
-            sent[j, pl.ds(16, 8), :] = jnp.where(low, four, tail)
+    strips = [surf_rows[pl.ds(f * 16 + x, 4, stride=4), :] for f in range(2) for x in range(4)]
+    for g, strip in enumerate(exchange(strips, lanes[0:4])):
+        for yb in range(4):
+            sent[pl.ds((yb * 8 + g) * SEND + 16, 1), :] = strip[yb : yb + 1, :]
     width = window.shape[0]
     start = jnp.min(cells[...] % width, axis=0, keepdims=True)
     place = lax.broadcasted_iota(jnp.int32, (width, 128), 0)
@@ -347,34 +361,46 @@
         block = pl.ds(v * 128, 128)
         levels[block, :] = turned[block, :].T
 
-    for v in range(8):
-        line = [surf_rows[pl.ds(v * 4 + x, 1), :] for x in range(4)]
-        steps = [(line[x] + line[x + 1]) * 0.5 for x in range(3)]
-        for zp in range(4):
-            j = v * 4 + zp
-            rate = rate_x * scales[zp]
-            e01, e12, e23 = (rate * step for step in steps)
-            rhs = [levels[pl.ds(v * 128 + zp * 32 + x, 8, stride=4), :] for x in range(4)]
-            one = rhs[1] * kept[j, pl.ds(0, 8), :]
-            two = (rhs[2] + e12 * one) * kept[j, pl.ds(24, 8), :]
-            one_upper = kept[j, pl.ds(16, 8), :]
-            sent[j, pl.ds(0, 8), :] = rhs[0] + (e01 + wind_x) * (one + one_upper * two)
-            sent[j, pl.ds(8, 8), :] = rhs[3] + e23 * two
-            kept[j, pl.ds(0, 8), :] = one
-            kept[j, pl.ds(24, 8), :] = two
-
-
-def middle_kernel(vectors, got, ends):
-    rows = sublane()
-    scale = jnp.where(rows < 4, got[0, pl.ds(20, 1), :], got[0, pl.ds(21, 1), :])
-    rate = vectors[0] * scale
+    for yb in range(4):
+        firsts, lasts = [], []
+        for f in range(2):
+            v = f * 4 + yb
+            line = [surf_rows[pl.ds(v * 4 + x, 1), :] for x in range(4)]
+            steps = [(line[x] + line[x + 1]) * 0.5 for x in range(3)]
+            for zp in range(4):
+                j = v * 4 + zp
+                rate = rate_x * scales[zp]
+                e01, e12, e23 = (rate * step for step in steps)
+                rhs = [levels[pl.ds(v * 128 + zp * 32 + x, 8, stride=4), :] for x in range(4)]
+                one = rhs[1] * kept[j, pl.ds(0, 8), :]
+                two = (rhs[2] + e12 * one) * kept[j, pl.ds(24, 8), :]
+                one_upper = kept[j, pl.ds(16, 8), :]
+                firsts.append(rhs[0] + (e01 + wind_x) * (one + one_upper * two))
+                lasts.append(rhs[3] + e23 * two)
+                kept[j, pl.ds(0, 8), :] = one
+                kept[j, pl.ds(24, 8), :] = two
+        for offset, items in ((0, firsts), (8, lasts)):
+            for g, item in enumerate(exchange(items, lanes)):
+                sent[pl.ds((yb * 8 + g) * SEND + offset, 8), :] = item
+
+
+def middle_kernel(vectors, got, ends, spread):
+    lanes = lane()
+    slabs = ends.shape[0]
+    for q in range(slabs // 8):
+        strip = got[pl.ds(q * 8 * SEND + 16, 8, stride=SEND), :]
+        turned = {d: pltpu.roll(strip, 16 * d % 128, axis=1) if d else strip for d in range(-3, 4)}
+        for x in range(4):
+            spread[pl.ds(x * slabs + q * 8, 8), :] = choose(
+                lanes // 16 % 4, [turned[zp - x] for zp in range(4)]
+            )
+    rate = vectors[0]
     wind = vectors[1]
-    slabs = got.shape[0]
     below, above, slack, rhs = [], [], [], []
     line = None
     outer = None
     for k in range(slabs):
-        line = [got[k, pl.ds(16 + x, 1), :] for x in range(4)]
+        line = [spread[pl.ds(x * slabs + k, 1), :] for x in range(4)]
         if k == 0:
             outer = rate * (line[0] * 0.5)
         e01, e12, e23 = (rate * ((line[x] + line[x + 1]) * 0.5) for x in range(3))
@@ -391,9 +417,9 @@
             below.append(outer)
         above.append(q0 * (one_upper * (two_next * two_inv)))
         slack.append(own)
-        rhs.append(got[k, pl.ds(0, 8), :])
+        rhs.append(got[pl.ds(k * SEND, 8), :])
         if k < slabs - 1:
-            outer = rate * ((line[3] + got[k + 1, pl.ds(16, 1), :]) * 0.5)
+            outer = rate * ((line[3] + spread[pl.ds(k + 1, 1), :]) * 0.5)
         else:
             outer = rate * (line[3] * 0.5)
         own = 1.0 + e23 * two_slack
@@ -404,7 +430,7 @@
             own = own + (outer + wind)
             above.append(None)
         slack.append(own)
-        rhs.append(got[k, pl.ds(8, 8), :])
+        rhs.append(got[pl.ds(k * SEND + 8, 8), :])
 
     def total(i):
         out = slack[i]
@@ -467,12 +493,18 @@
     return first, one, two, last
 
 
-def sums_kernel(vectors, window, ends, kept, grad):
+def sums_kernel(vectors, window, ends, kept, grad, sorted_ends):
     parts = []
+    lanes = lane()
+    for yb in range(4):
+        for row in (0, 8):
+            items = exchange([ends[yb * 8 + g, pl.ds(row, 8), :] for g in range(8)], lanes)
+            for m, item in enumerate(items):
+                sorted_ends[(m // 4 * 4 + yb) * 4 + m % 4, pl.ds(row, 8), :] = item
     for v in range(8):
         total = None
         for zp in range(4):
-            first, one, two, last = inner_rows(ends, kept, v * 4 + zp)
+            first, one, two, last = inner_rows(sorted_ends, kept, v * 4 + zp)
             item = vectors[2 + (v // 4) * 4 + zp] * ((first + one) + (two + last))
             total = item if total is None else total + item
         parts.append(jnp.sum(total, axis=0, keepdims=True))
@@ -527,7 +559,7 @@
     sent, kept, vectors, window = pl.pallas_call(
         first_kernel,
         out_shape=(
-            jax.ShapeDtypeStruct((slabs, SEND, 128), F32),
+            jax.ShapeDtypeStruct((slabs * SEND, 128), F32),
             jax.ShapeDtypeStruct((slabs, 48, 128), F32),
             jax.ShapeDtypeStruct((10, 8, 128), F32),
             jax.ShapeDtypeStruct((width, cells.shape[1]), jnp.bfloat16),
@@ -540,20 +572,24 @@
         + [pltpu.VMEM((32, 128), F32), pltpu.SemaphoreType.DMA((9,))],
         compiler_params=params,
     )(*(pltpu.with_memory_space_constraint(item, pltpu.HBM) for item in operands))
-    got = lax.all_to_all(sent, "tile", 0, 0)
+    got = lax.all_to_all(sent.reshape(slabs, SEND, 1, 128), "tile", 0, 0).reshape(slabs * SEND, 128)
     ends = pl.pallas_call(
         middle_kernel,
         out_shape=jax.ShapeDtypeStruct((slabs, 16, 128), F32),
         in_specs=[vmem] * 2,
         out_specs=vmem,
+        scratch_shapes=[pltpu.VMEM((4 * slabs, 128), F32)],
         compiler_params=params,
     )(vectors, got)
     ends = lax.all_to_all(ends, "tile", 0, 0)
-    grad = pl.pallas_call(
+    grad, ends = pl.pallas_call(
         sums_kernel,
-        out_shape=jax.ShapeDtypeStruct((2, cells.shape[1]), F32),
+        out_shape=(
+            jax.ShapeDtypeStruct((2, cells.shape[1]), F32),
+            jax.ShapeDtypeStruct((slabs, 16, 128), F32),
+        ),
         in_specs=[vmem] * 4,
-        out_specs=vmem,
+        out_specs=(vmem, vmem),
         compiler_params=params,
     )(vectors, window, ends, kept)
     state = pl.pallas_call(
@@ -564,11 +600,12 @@
         scratch_shapes=[pltpu.VMEM((1024, 128), F32)],
         compiler_params=params,
     )(ends, kept)
-    grad = grad + lax.ppermute(grad, "scen", [(i, i ^ 1) for i in range(groups)])
-    grad = grad + sum(
-        lax.ppermute(grad, "scen", [(i, (i + step) % groups) for i in range(groups)])
-        for step in (2, 6, 4)
-    )
+    for partner in (
+        lambda i: i ^ 1,
+        lambda i: i ^ 2,
+        lambda i: groups - 2 - i + 2 * (i % 2),
+    ):
+        grad = grad + lax.ppermute(grad, "scen", [(i, partner(i)) for i in range(groups)])
     state = state.reshape(4, 2, 8, 4, 4, 128).transpose(0, 1, 2, 4, 3, 5).reshape(cotangent.shape)
     return (state, grad)
 

time: 57.8 us -> 55.8 us (0.965)
  the two profiles are of different devices: /device:TPU:1 before, /device:TPU:24 now
where the time goes in v3:
time: 55.8 us; the launch traced here: 55.7 us
  blocking collectives  40.4 us (72%)
  waiting for transfers between devices  7.64 us (14%)
  Pallas kernels  5.43 us (10%)
  starting transfers between devices  0.97 us (2%)
  between operations  0.65 us (1%)
  other arithmetic  0.57 us (1%)
    all_to_all x1, blocking collectives, on_device(): lax.all_to_all(sent.reshape(slabs, SEND, 1, 128), 'tile', 0, 0)  24.1 us
    all_to_all x1, blocking collectives, on_device(): ends = lax.all_to_all(ends, 'tile', 0, 0)  16.3 us
    ppermute x3, waiting for transfers between devices, on_device(): lax.ppermute(grad, 'scen', [(i, partner(i)) for i in range(groups)])  7.64 us
    pallas_call x1, Pallas kernels, on_device(): pl.pallas_call(first_kernel, out_shape=(jax.ShapeDtypeStruct((slabs * SEN...  3.45 us
  transfers between devices with their start and end apart: 3, of which 3 were waited for; matrix products, arithmetic and copies ran while one was open for 0% of the time, Pallas kernels for 2%

profile of v3, /device:TPU:24, one launch (start us, length us, event | category | flops | bytes accessed | tf_op | source)
XLA Modules:
  0.0 55.7 jit_solution(8564291978755348335)
XLA Ops:
  0.6 3.5 %shard_map.95 = (f32[544,128]{1,0:T(8,128)S(1)}, f32[32,48,128]{2,1,0:T(8,128)S(1)}, f32[10,8,128]{2,1,0:T(8,128)S(1)}, bf16[512,128]{1,0:T(8,128)(2,1)S(1)}) custom-call(s32[4]{0:T(128)} %ids_in.1, f32[8,64]{1,0:T(8,128)} %bitcast.25, f32[2,17]{1,0:T(2,128)} %class_diff_in.1, f32[8]{0:T(128)} %scale_in.1, f32[8]{0:T(128)} %emit_in.1, s32[16,128]{1,0:T(8,128)} %bitcast.23, ...), custom_call_target="tpu_custom_call" | custom-call | tf_op jit(solution)/shard_map/pallas_call | solution.py:559
  4.1 24.1 %all_to_all.10 = f32[32,17,1,128]{3,2,1,0:T(1,128)S(1)} all-to-all(f32[32,17,1,128]{3,2,1,0:T(1,128)S(1)} %bitcast.20), channel_id=1, replica_groups=mesh['scen'=8,'tile'=32] {'tile'}, dimensions={0} | all-to-all | bytes 557056 | tf_op jit(solution)/shard_map/all_to_all | solution.py:575
  28.2 0.6 %shard_map.96 = f32[32,16,128]{2,1,0:T(8,128)S(1)} custom-call(f32[10,8,128]{2,1,0:T(8,128)S(1)} %get-tuple-element.8.vectors, f32[544,128]{1,0:T(8,128)S(1)} %bitcast.19), custom_call_target="tpu_custom_call" | custom-call | tf_op jit(solution)/shard_map/pallas_call | solution.py:576
  28.8 16.3 %all_to_all.11.ends = f32[32,16,128]{2,1,0:T(8,128)S(1)} all-to-all(f32[32,16,128]{2,1,0:T(8,128)S(1)} %shard_map.96), channel_id=1, replica_groups=mesh['scen'=8,'tile'=32] {'tile'}, dimensions={0} | all-to-all | bytes 524288 | tf_op jit(solution)/shard_map/all_to_all | solution.py:584
  45.1 0.4 shard_map.97
  45.6 0.0 collective-permute-start
  45.6 1.1 %collective-permute-done = f32[2,128]{1,0:T(2,128)S(1)} collective-permute-done((f32[2,128]{1,0:T(2,128)S(1)}, f32[2,128]{1,0:T(2,128)S(1)}, u32[]{:S(2)}, u32[]{:S(2)}) %collective-permute-start) | collective-permute-done | bytes 1056 | tf_op jit(solution)/shard_map/ppermute | solution.py:608
  46.7 0.7 %collective-permute-start.1 = (f32[2,128]{1,0:T(2,128)S(1)}, f32[2,128]{1,0:T(2,128)S(1)}, u32[]{:S(2)}, u32[]{:S(2)}) collective-permute-start(f32[2,128]{1,0:T(2,128)S(1)} %add.9), channel_id=1, source_target_pairs={{0,64},{32,96},{64,0},{96,32},{128,192},{160,224},{192,128},{224,1... | collective-permute-start | bytes 3080 | tf_op jit(solution)/shard_map/ppermute | solution.py:608
  47.5 2.8 %collective-permute-done.1 = f32[2,128]{1,0:T(2,128)S(1)} collective-permute-done((f32[2,128]{1,0:T(2,128)S(1)}, f32[2,128]{1,0:T(2,128)S(1)}, u32[]{:S(2)}, u32[]{:S(2)}) %collective-permute-start.1) | collective-permute-done | bytes 1056 | tf_op jit(solution)/shard_map/ppermute | solution.py:608
  50.3 0.2 collective-permute-start.2
  50.5 0.9 %shard_map.98 = f32[1024,128]{1,0:T(8,128)} custom-call(f32[32,16,128]{2,1,0:T(8,128)S(1)} %get-tuple-element.12.ends, f32[32,48,128]{2,1,0:T(8,128)S(1)} %get-tuple-element.11.kept), custom_call_target="tpu_custom_call" | custom-call | tf_op jit(solution)/shard_map/pallas_call | solution.py:595
  51.4 3.7 %collective-permute-done.2 = f32[2,128]{1,0:T(2,128)S(1)} collective-permute-done((f32[2,128]{1,0:T(2,128)S(1)}, f32[2,128]{1,0:T(2,128)S(1)}, u32[]{:S(2)}, u32[]{:S(2)}) %collective-permute-start.2) | collective-permute-done | bytes 1056 | tf_op jit(solution)/shard_map/ppermute | solution.py:608
  55.1 0.6 %add.11 = f32[2,128]{1,0:T(2,128)} add(f32[2,128]{1,0:T(2,128)S(1)} %add.10, f32[2,128]{1,0:T(2,128)S(1)} %collective-permute-done.2) | non-fusion elementwise | flops 256 | bytes 3072 | tf_op jit(solution)/shard_map/add | solution.py:608
  (2 shorter events, 0.0 us)
Async XLA Ops:
  45.6 1.1 %collective-permute-start = (f32[2,128]{1,0:T(2,128)S(1)}, f32[2,128]{1,0:T(2,128)S(1)}, u32[]{:S(2)}, u32[]{:S(2)}) collective-permute-start(f32[2,128]{1,0:T(2,128)S(1)} %get-tuple-element.13), channel_id=1, source_target_pairs={{0,32},{32,0},{64,96},{96,64},{128,160},{160,128},{192,224},{224,1... | collective-permute-start | bytes 3080 | tf_op jit(solution)/shard_map/ppermute | solution.py:608
  46.7 3.6 %collective-permute-start.1 = (f32[2,128]{1,0:T(2,128)S(1)}, f32[2,128]{1,0:T(2,128)S(1)}, u32[]{:S(2)}, u32[]{:S(2)}) collective-permute-start(f32[2,128]{1,0:T(2,128)S(1)} %add.9), channel_id=1, source_target_pairs={{0,64},{32,96},{64,0},{96,32},{128,192},{160,224},{192,128},{224,1... | collective-permute-start | bytes 3080 | tf_op jit(solution)/shard_map/ppermute | solution.py:608
  50.3 4.8 %collective-permute-start.2 = (f32[2,128]{1,0:T(2,128)S(1)}, f32[2,128]{1,0:T(2,128)S(1)}, u32[]{:S(2)}, u32[]{:S(2)}) collective-permute-start(f32[2,128]{1,0:T(2,128)S(1)} %add.10), channel_id=1, source_target_pairs={{0,192},{32,224},{64,128},{96,160},{128,64},{160,96},{192,0},{224,... | collective-permute-start | bytes 3080 | tf_op jit(solution)/shard_map/ppermute | solution.py:608

commit v4 on v3

--- a/solution.py
+++ b/solution.py
@@ -10,9 +10,7 @@
 
 
 def inverse(value):
-    guess = pl.reciprocal(value, approx=True)
-    guess = guess * (2.0 - value * guess)
-    return guess * (2.0 - value * guess)
+    return pltpu.reciprocal(value, approx=True)
 
 
 def sublane():
@@ -48,18 +46,21 @@
     )
 
 
-def exchange(items, lanes):
-    for bit in range(3):
-        step = 1 << bit
-        clear = (lanes // 16) // step % 2 == 0
-        out = list(items)
-        for n in range(8):
-            if n & step == 0:
-                first, second = items[n], items[n + step]
-                out[n] = jnp.where(clear, first, pltpu.roll(second, 16 * step, axis=1))
-                out[n + step] = jnp.where(clear, pltpu.roll(first, 128 - 16 * step, axis=1), second)
-        items = out
-    return items
+def pick(groups, items):
+    out = items[3]
+    for at in range(2, -1, -1):
+        out = jnp.where(groups == at, items[at], out)
+    return out
+
+
+def to_strips(items, groups):
+    turned = [pltpu.roll(item, 32 * m, axis=1) if m else item for m, item in enumerate(items)]
+    return [pick(groups, [turned[(p - g) % 4] for p in range(4)]) for g in range(4)]
+
+
+def from_strips(strips, groups):
+    items = [pick(groups, [strips[(p - m) % 4] for p in range(4)]) for m in range(4)]
+    return [pltpu.roll(item, 128 - 32 * m, axis=1) if m else item for m, item in enumerate(items)]
 
 
 def solve_levels(cot, surf, scale, table, out, hold_a, hold_c, low, arrivals):
@@ -324,12 +325,14 @@
     rate_x = choose(rows % 4, [table(s, 0) for s in range(4)])
     wind_x = choose(rows % 4, [table(s, 3) for s in range(4)])
     scales = [choose(rows // 4, [scale[2 * zp], scale[2 * zp + 1]]) for zp in range(4)]
-    vectors[0] = rate_x * choose(lanes // 16 % 4, scales)
-    vectors[1] = wind_x
+    groups = lanes // 32
+    for g in range(4):
+        vectors[g] = rate_x * choose(groups, [scales[(p - g) % 4] for p in range(4)])
+    vectors[4] = wind_x
     for f in range(2):
         factor = choose(rows % 4, [table(s, 6 + f) for s in range(4)])
         for zp in range(4):
-            vectors[2 + f * 4 + zp] = factor * choose(rows // 4, [emit[2 * zp], emit[2 * zp + 1]])
+            vectors[5 + f * 4 + zp] = factor * choose(rows // 4, [emit[2 * zp], emit[2 * zp + 1]])
     for v in range(8):
         line = [surf_rows[pl.ds(v * 4 + x, 1), :] for x in range(4)]
         steps = [(line[x] + line[x + 1]) * 0.5 for x in range(3)]
@@ -343,10 +346,14 @@
                 (one_inv, one_fill, one_upper, two_inv, two_fill * two_inv, two_next * two_inv)
             ):
                 kept[j, pl.ds(n * 8, 8), :] = item
-    strips = [surf_rows[pl.ds(f * 16 + x, 4, stride=4), :] for f in range(2) for x in range(4)]
-    for g, strip in enumerate(exchange(strips, lanes[0:4])):
-        for yb in range(4):
-            sent[pl.ds((yb * 8 + g) * SEND + 16, 1), :] = strip[yb : yb + 1, :]
+    lines = [surf_rows[pl.ds(x, 8, stride=4), :] for x in range(4)]
+    lines = [
+        [pltpu.roll(item, 32 * d, axis=1) if d else item for d in range(4)] for item in lines
+    ]
+    strips = [pick(groups, [lines[x][(x - g) % 4] for x in range(4)]) for g in range(4)]
+    for g in range(4):
+        for v in range(8):
+            sent[pl.ds((v * 4 + g) * SEND + 16, 1), :] = strips[g][v : v + 1, :]
     width = window.shape[0]
     start = jnp.min(cells[...] % width, axis=0, keepdims=True)
     place = lax.broadcasted_iota(jnp.int32, (width, 128), 0)
@@ -361,41 +368,40 @@
         block = pl.ds(v * 128, 128)
         levels[block, :] = turned[block, :].T
 
-    for yb in range(4):
+    for v in range(8):
+        line = [surf_rows[pl.ds(v * 4 + x, 1), :] for x in range(4)]
+        steps = [(line[x] + line[x + 1]) * 0.5 for x in range(3)]
         firsts, lasts = [], []
-        for f in range(2):
-            v = f * 4 + yb
-            line = [surf_rows[pl.ds(v * 4 + x, 1), :] for x in range(4)]
-            steps = [(line[x] + line[x + 1]) * 0.5 for x in range(3)]
-            for zp in range(4):
-                j = v * 4 + zp
-                rate = rate_x * scales[zp]
-                e01, e12, e23 = (rate * step for step in steps)
-                rhs = [levels[pl.ds(v * 128 + zp * 32 + x, 8, stride=4), :] for x in range(4)]
-                one = rhs[1] * kept[j, pl.ds(0, 8), :]
-                two = (rhs[2] + e12 * one) * kept[j, pl.ds(24, 8), :]
-                one_upper = kept[j, pl.ds(16, 8), :]
-                firsts.append(rhs[0] + (e01 + wind_x) * (one + one_upper * two))
-                lasts.append(rhs[3] + e23 * two)
-                kept[j, pl.ds(0, 8), :] = one
-                kept[j, pl.ds(24, 8), :] = two
+        for zp in range(4):
+            j = v * 4 + zp
+            rate = rate_x * scales[zp]
+            e01, e12, e23 = (rate * step for step in steps)
+            rhs = [levels[pl.ds(v * 128 + zp * 32 + x, 8, stride=4), :] for x in range(4)]
+            one = rhs[1] * kept[j, pl.ds(0, 8), :]
+            two = (rhs[2] + e12 * one) * kept[j, pl.ds(24, 8), :]
+            one_upper = kept[j, pl.ds(16, 8), :]
+            firsts.append(rhs[0] + (e01 + wind_x) * (one + one_upper * two))
+            lasts.append(rhs[3] + e23 * two)
+            kept[j, pl.ds(0, 8), :] = one
+            kept[j, pl.ds(24, 8), :] = two
         for offset, items in ((0, firsts), (8, lasts)):
-            for g, item in enumerate(exchange(items, lanes)):
-                sent[pl.ds((yb * 8 + g) * SEND + offset, 8), :] = item
+            for g, item in enumerate(to_strips(items, groups)):
+                sent[pl.ds((v * 4 + g) * SEND + offset, 8), :] = item
 
 
 def middle_kernel(vectors, got, ends, spread):
-    lanes = lane()
+    groups = lane() // 32
     slabs = ends.shape[0]
+    strip = lax.axis_index("tile") % 4
     for q in range(slabs // 8):
-        strip = got[pl.ds(q * 8 * SEND + 16, 8, stride=SEND), :]
-        turned = {d: pltpu.roll(strip, 16 * d % 128, axis=1) if d else strip for d in range(-3, 4)}
+        shared = got[pl.ds(q * 8 * SEND + 16, 8, stride=SEND), :]
+        turned = [pltpu.roll(shared, 32 * d, axis=1) if d else shared for d in range(4)]
         for x in range(4):
-            spread[pl.ds(x * slabs + q * 8, 8), :] = choose(
-                lanes // 16 % 4, [turned[zp - x] for zp in range(4)]
+            spread[pl.ds(x * slabs + q * 8, 8), :] = pick(
+                groups, [turned[(p - x) % 4] for p in range(4)]
             )
-    rate = vectors[0]
-    wind = vectors[1]
+    rate = vectors[strip]
+    wind = vectors[4]
     below, above, slack, rhs = [], [], [], []
     line = None
     outer = None
@@ -495,17 +501,17 @@
 
 def sums_kernel(vectors, window, ends, kept, grad, sorted_ends):
     parts = []
-    lanes = lane()
-    for yb in range(4):
+    groups = lane() // 32
+    for v in range(8):
         for row in (0, 8):
-            items = exchange([ends[yb * 8 + g, pl.ds(row, 8), :] for g in range(8)], lanes)
-            for m, item in enumerate(items):
-                sorted_ends[(m // 4 * 4 + yb) * 4 + m % 4, pl.ds(row, 8), :] = item
+            items = from_strips([ends[v * 4 + g, pl.ds(row, 8), :] for g in range(4)], groups)
+            for zp, item in enumerate(items):
+                sorted_ends[v * 4 + zp, pl.ds(row, 8), :] = item
     for v in range(8):
         total = None
         for zp in range(4):
             first, one, two, last = inner_rows(sorted_ends, kept, v * 4 + zp)
-            item = vectors[2 + (v // 4) * 4 + zp] * ((first + one) + (two + last))
+            item = vectors[5 + (v // 4) * 4 + zp] * ((first + one) + (two + last))
             total = item if total is None else total + item
         parts.append(jnp.sum(total, axis=0, keepdims=True))
     sums = [jnp.concatenate(parts[f * 4 : f * 4 + 4], axis=1) for f in range(2)]
@@ -561,7 +567,7 @@
         out_shape=(
             jax.ShapeDtypeStruct((slabs * SEND, 128), F32),
             jax.ShapeDtypeStruct((slabs, 48, 128), F32),
-            jax.ShapeDtypeStruct((10, 8, 128), F32),
+            jax.ShapeDtypeStruct((13, 8, 128), F32),
             jax.ShapeDtypeStruct((width, cells.shape[1]), jnp.bfloat16),
         ),
         in_specs=[hbm] * 8,

time: 55.8 us -> 54.8 us (0.982)
  Pallas kernels: 5.43 us -> 4.37 us
    pallas_call x1, Pallas kernels: 3.45 us -> 2.7 us  [on_device(): pl.pallas_call(first_kernel, out_shape=(jax.ShapeDtypeStruct((slabs * SEN...]
where the time goes in v4:
time: 54.8 us; the launch traced here: 54.6 us
  blocking collectives  40.4 us (74%)
  waiting for transfers between devices  7.63 us (14%)
  Pallas kernels  4.37 us (8%)
  starting transfers between devices  0.97 us (2%)
  between operations  0.66 us (1%)
  other arithmetic  0.57 us (1%)
    all_to_all x1, blocking collectives, on_device(): lax.all_to_all(sent.reshape(slabs, SEND, 1, 128), 'tile', 0, 0)  24.1 us
    all_to_all x1, blocking collectives, on_device(): ends = lax.all_to_all(ends, 'tile', 0, 0)  16.3 us
    ppermute x3, waiting for transfers between devices, on_device(): lax.ppermute(grad, 'scen', [(i, partner(i)) for i in range(groups)])  7.63 us
    pallas_call x1, Pallas kernels, on_device(): pl.pallas_call(first_kernel, out_shape=(jax.ShapeDtypeStruct((slabs * SEN...  2.7 us
  transfers between devices with their start and end apart: 3, of which 3 were waited for; matrix products, arithmetic and copies ran while one was open for 0% of the time, Pallas kernels for 2%

profile of v4, /device:TPU:24, one launch (start us, length us, event | category | flops | bytes accessed | tf_op | source)
XLA Modules:
  0.0 54.6 jit_solution(12855649509683396785)
XLA Ops:
  0.6 2.7 %shard_map.95 = (f32[544,128]{1,0:T(8,128)S(1)}, f32[32,48,128]{2,1,0:T(8,128)S(1)}, f32[13,8,128]{2,1,0:T(8,128)S(1)}, bf16[512,128]{1,0:T(8,128)(2,1)S(1)}) custom-call(s32[4]{0:T(128)} %ids_in.1, f32[8,64]{1,0:T(8,128)} %bitcast.25, f32[2,17]{1,0:T(2,128)} %class_diff_in.1, f32[8]{0:T(128)} %scale_in.1, f32[8]{0:T(128)} %emit_in.1, s32[16,128]{1,0:T(8,128)} %bitcast.23, ...), custom_call_target="tpu_custom_call" | custom-call | tf_op jit(solution)/shard_map/pallas_call | solution.py:565
  3.3 24.1 %all_to_all.10 = f32[32,17,1,128]{3,2,1,0:T(1,128)S(1)} all-to-all(f32[32,17,1,128]{3,2,1,0:T(1,128)S(1)} %bitcast.20), channel_id=1, replica_groups=mesh['scen'=8,'tile'=32] {'tile'}, dimensions={0} | all-to-all | bytes 557056 | tf_op jit(solution)/shard_map/all_to_all | solution.py:581
  27.4 0.5 shard_map.96
  27.9 16.3 %all_to_all.11.ends = f32[32,16,128]{2,1,0:T(8,128)S(1)} all-to-all(f32[32,16,128]{2,1,0:T(8,128)S(1)} %shard_map.96), channel_id=1, replica_groups=mesh['scen'=8,'tile'=32] {'tile'}, dimensions={0} | all-to-all | bytes 524288 | tf_op jit(solution)/shard_map/all_to_all | solution.py:590
  44.2 0.3 shard_map.97
  44.5 0.0 collective-permute-start
  44.5 1.1 %collective-permute-done = f32[2,128]{1,0:T(2,128)S(1)} collective-permute-done((f32[2,128]{1,0:T(2,128)S(1)}, f32[2,128]{1,0:T(2,128)S(1)}, u32[]{:S(2)}, u32[]{:S(2)}) %collective-permute-start) | collective-permute-done | bytes 1056 | tf_op jit(solution)/shard_map/ppermute | solution.py:614
  45.7 0.7 %collective-permute-start.1 = (f32[2,128]{1,0:T(2,128)S(1)}, f32[2,128]{1,0:T(2,128)S(1)}, u32[]{:S(2)}, u32[]{:S(2)}) collective-permute-start(f32[2,128]{1,0:T(2,128)S(1)} %add.9), channel_id=1, source_target_pairs={{0,64},{32,96},{64,0},{96,32},{128,192},{160,224},{192,128},{224,1... | collective-permute-start | bytes 3080 | tf_op jit(solution)/shard_map/ppermute | solution.py:614
  46.4 2.8 %collective-permute-done.1 = f32[2,128]{1,0:T(2,128)S(1)} collective-permute-done((f32[2,128]{1,0:T(2,128)S(1)}, f32[2,128]{1,0:T(2,128)S(1)}, u32[]{:S(2)}, u32[]{:S(2)}) %collective-permute-start.1) | collective-permute-done | bytes 1056 | tf_op jit(solution)/shard_map/ppermute | solution.py:614
  49.2 0.2 collective-permute-start.2
  49.5 0.9 %shard_map.98 = f32[1024,128]{1,0:T(8,128)} custom-call(f32[32,16,128]{2,1,0:T(8,128)S(1)} %get-tuple-element.12.ends, f32[32,48,128]{2,1,0:T(8,128)S(1)} %get-tuple-element.11.kept), custom_call_target="tpu_custom_call" | custom-call | tf_op jit(solution)/shard_map/pallas_call | solution.py:601
  50.4 3.7 %collective-permute-done.2 = f32[2,128]{1,0:T(2,128)S(1)} collective-permute-done((f32[2,128]{1,0:T(2,128)S(1)}, f32[2,128]{1,0:T(2,128)S(1)}, u32[]{:S(2)}, u32[]{:S(2)}) %collective-permute-start.2) | collective-permute-done | bytes 1056 | tf_op jit(solution)/shard_map/ppermute | solution.py:614
  54.0 0.6 %add.11 = f32[2,128]{1,0:T(2,128)} add(f32[2,128]{1,0:T(2,128)S(1)} %add.10, f32[2,128]{1,0:T(2,128)S(1)} %collective-permute-done.2) | non-fusion elementwise | flops 256 | bytes 3072 | tf_op jit(solution)/shard_map/add | solution.py:614
  (2 shorter events, 0.0 us)
Async XLA Ops:
  44.5 1.1 %collective-permute-start = (f32[2,128]{1,0:T(2,128)S(1)}, f32[2,128]{1,0:T(2,128)S(1)}, u32[]{:S(2)}, u32[]{:S(2)}) collective-permute-start(f32[2,128]{1,0:T(2,128)S(1)} %get-tuple-element.13), channel_id=1, source_target_pairs={{0,32},{32,0},{64,96},{96,64},{128,160},{160,128},{192,224},{224,1... | collective-permute-start | bytes 3080 | tf_op jit(solution)/shard_map/ppermute | solution.py:614
  45.7 3.6 %collective-permute-start.1 = (f32[2,128]{1,0:T(2,128)S(1)}, f32[2,128]{1,0:T(2,128)S(1)}, u32[]{:S(2)}, u32[]{:S(2)}) collective-permute-start(f32[2,128]{1,0:T(2,128)S(1)} %add.9), channel_id=1, source_target_pairs={{0,64},{32,96},{64,0},{96,32},{128,192},{160,224},{192,128},{224,1... | collective-permute-start | bytes 3080 | tf_op jit(solution)/shard_map/ppermute | solution.py:614
  49.2 4.8 %collective-permute-start.2 = (f32[2,128]{1,0:T(2,128)S(1)}, f32[2,128]{1,0:T(2,128)S(1)}, u32[]{:S(2)}, u32[]{:S(2)}) collective-permute-start(f32[2,128]{1,0:T(2,128)S(1)} %add.10), channel_id=1, source_target_pairs={{0,192},{32,224},{64,128},{96,160},{128,64},{160,96},{192,0},{224,... | collective-permute-start | bytes 3080 | tf_op jit(solution)/shard_map/ppermute | solution.py:614

commit v5 on v4

--- a/solution.py
+++ b/solution.py
@@ -606,12 +606,11 @@
         scratch_shapes=[pltpu.VMEM((1024, 128), F32)],
         compiler_params=params,
     )(ends, kept)
-    for partner in (
-        lambda i: i ^ 1,
-        lambda i: i ^ 2,
-        lambda i: groups - 2 - i + 2 * (i % 2),
-    ):
-        grad = grad + lax.ppermute(grad, "scen", [(i, partner(i)) for i in range(groups)])
+    grad = grad + lax.ppermute(grad, "scen", [(i, i ^ 1) for i in range(groups)])
+    shifted = [
+        lax.ppermute(grad, "scen", [(i, i ^ step) for i in range(groups)]) for step in (2, 4, 6)
+    ]
+    grad = (grad + shifted[0]) + (shifted[1] + shifted[2])
     state = state.reshape(4, 2, 8, 4, 4, 128).transpose(0, 1, 2, 4, 3, 5).reshape(cotangent.shape)
     return (state, grad)
 

time: 54.8 us -> 54.3 us (level)
  the two profiles are of different devices: /device:TPU:24 before, /device:TPU:1 now
where the time goes in v5:
time: 54.3 us; the launch traced here: 54.1 us
  blocking collectives  38.1 us (70%)
  starting transfers between devices  7.08 us (13%)
  Pallas kernels  4.37 us (8%)
  waiting for transfers between devices  3.27 us (6%)
  between operations  0.66 us (1%)
  other arithmetic  0.57 us (1%)
    all_to_all x1, blocking collectives, on_device(): lax.all_to_all(sent.reshape(slabs, SEND, 1, 128), 'tile', 0, 0)  23.5 us
    all_to_all x1, blocking collectives, on_device(): ends = lax.all_to_all(ends, 'tile', 0, 0)  14.7 us
    ppermute x1, starting transfers between devices, on_device(): lax.ppermute(grad, 'scen', [(i, i ^ 1) for i in range(groups)])  3.76 us
    ppermute x3, starting transfers between devices, on_device(): lax.ppermute(grad, 'scen', [(i, i ^ step) for i in range(groups)])  3.31 us
    pallas_call x1, Pallas kernels, on_device(): pl.pallas_call(first_kernel, out_shape=(jax.ShapeDtypeStruct((slabs * SEN...  2.7 us
    ppermute x3, waiting for transfers between devices, on_device(): lax.ppermute(grad, 'scen', [(i, i ^ step) for i in range(groups)])  2.45 us
  transfers between devices with their start and end apart: 4, of which 2 were waited for; matrix products, arithmetic and copies ran while one was open for 0% of the time, Pallas kernels for 2%

profile of v5, /device:TPU:1, one launch (start us, length us, event | category | flops | bytes accessed | tf_op | source)
XLA Modules:
  0.0 54.1 jit_solution(7118806514070311831)
XLA Ops:
  0.6 2.7 %shard_map.95 = (f32[544,128]{1,0:T(8,128)S(1)}, f32[32,48,128]{2,1,0:T(8,128)S(1)}, f32[13,8,128]{2,1,0:T(8,128)S(1)}, bf16[512,128]{1,0:T(8,128)(2,1)S(1)}) custom-call(s32[4]{0:T(128)} %ids_in.1, f32[8,64]{1,0:T(8,128)} %bitcast.25, f32[2,17]{1,0:T(2,128)} %class_diff_in.1, f32[8]{0:T(128)} %scale_in.1, f32[8]{0:T(128)} %emit_in.1, s32[16,128]{1,0:T(8,128)} %bitcast.23, ...), custom_call_target="tpu_custom_call" | custom-call | tf_op jit(solution)/shard_map/pallas_call | solution.py:565
  3.3 23.5 %all_to_all.10 = f32[32,17,1,128]{3,2,1,0:T(1,128)S(1)} all-to-all(f32[32,17,1,128]{3,2,1,0:T(1,128)S(1)} %bitcast.20), channel_id=1, replica_groups=mesh['scen'=8,'tile'=32] {'tile'}, dimensions={0} | all-to-all | bytes 557056 | tf_op jit(solution)/shard_map/all_to_all | solution.py:581
  26.8 0.5 shard_map.96
  27.3 14.7 %all_to_all.11.ends = f32[32,16,128]{2,1,0:T(8,128)S(1)} all-to-all(f32[32,16,128]{2,1,0:T(8,128)S(1)} %shard_map.96), channel_id=1, replica_groups=mesh['scen'=8,'tile'=32] {'tile'}, dimensions={0} | all-to-all | bytes 524288 | tf_op jit(solution)/shard_map/all_to_all | solution.py:590
  42.0 0.3 shard_map.97
  42.3 3.8 %collective-permute-start = (f32[2,128]{1,0:T(2,128)S(1)}, f32[2,128]{1,0:T(2,128)S(1)}, u32[]{:S(2)}, u32[]{:S(2)}) collective-permute-start(f32[2,128]{1,0:T(2,128)S(1)} %get-tuple-element.13), channel_id=1, source_target_pairs={{0,32},{32,0},{64,96},{96,64},{128,160},{160,128},{192,224},{224,1... | collective-permute-start | bytes 3080 | tf_op jit(solution)/shard_map/ppermute | solution.py:609
  46.0 0.8 %collective-permute-done = f32[2,128]{1,0:T(2,128)S(1)} collective-permute-done((f32[2,128]{1,0:T(2,128)S(1)}, f32[2,128]{1,0:T(2,128)S(1)}, u32[]{:S(2)}, u32[]{:S(2)}) %collective-permute-start) | collective-permute-done | bytes 1056 | tf_op jit(solution)/shard_map/ppermute | solution.py:609
  46.9 2.7 %collective-permute-start.3 = (f32[2,128]{1,0:T(2,128)S(1)}, f32[2,128]{1,0:T(2,128)S(1)}, u32[]{:S(2)}, u32[]{:S(2)}) collective-permute-start(f32[2,128]{1,0:T(2,128)S(1)} %add.12), channel_id=1, source_target_pairs={{0,192},{32,224},{64,128},{96,160},{128,64},{160,96},{192,0},{224,... | collective-permute-start | bytes 3080 | tf_op jit(solution)/shard_map/ppermute | solution.py:611
  49.6 0.3 collective-permute-start.2
  49.9 0.2 collective-permute-start.1
  50.2 0.9 %shard_map.98 = f32[1024,128]{1,0:T(8,128)} custom-call(f32[32,16,128]{2,1,0:T(8,128)S(1)} %get-tuple-element.12.ends, f32[32,48,128]{2,1,0:T(8,128)S(1)} %get-tuple-element.11.kept), custom_call_target="tpu_custom_call" | custom-call | tf_op jit(solution)/shard_map/pallas_call | solution.py:601
  51.1 0.0 collective-permute-done.3
  51.1 2.4 %collective-permute-done.2 = f32[2,128]{1,0:T(2,128)S(1)} collective-permute-done((f32[2,128]{1,0:T(2,128)S(1)}, f32[2,128]{1,0:T(2,128)S(1)}, u32[]{:S(2)}, u32[]{:S(2)}) %collective-permute-start.2) | collective-permute-done | bytes 1056 | tf_op jit(solution)/shard_map/ppermute | solution.py:611
  53.5 0.0 collective-permute-done.1
  53.5 0.6 %add_add_fusion = f32[2,128]{1,0:T(2,128)} fusion(f32[2,128]{1,0:T(2,128)S(1)} %collective-permute-done.2, f32[2,128]{1,0:T(2,128)S(1)} %collective-permute-done.3, f32[2,128]{1,0:T(2,128)S(1)} %add.12, f32[2,128]{1,0:T(2,128)S(1)} %collective-permute-done.1), kind=kLoop, calls=%fused_computation | loop fusion | flops 768 | bytes 5120 | tf_op jit(solution)/shard_map/add | solution.py:613
  (1 shorter events, 0.0 us)
Async XLA Ops:
  42.3 4.6 %collective-permute-start = (f32[2,128]{1,0:T(2,128)S(1)}, f32[2,128]{1,0:T(2,128)S(1)}, u32[]{:S(2)}, u32[]{:S(2)}) collective-permute-start(f32[2,128]{1,0:T(2,128)S(1)} %get-tuple-element.13), channel_id=1, source_target_pairs={{0,32},{32,0},{64,96},{96,64},{128,160},{160,128},{192,224},{224,1... | collective-permute-start | bytes 3080 | tf_op jit(solution)/shard_map/ppermute | solution.py:609
  46.9 4.2 %collective-permute-start.3 = (f32[2,128]{1,0:T(2,128)S(1)}, f32[2,128]{1,0:T(2,128)S(1)}, u32[]{:S(2)}, u32[]{:S(2)}) collective-permute-start(f32[2,128]{1,0:T(2,128)S(1)} %add.12), channel_id=1, source_target_pairs={{0,192},{32,224},{64,128},{96,160},{128,64},{160,96},{192,0},{224,... | collective-permute-start | bytes 3080 | tf_op jit(solution)/shard_map/ppermute | solution.py:611
  49.6 3.9 %collective-permute-start.2 = (f32[2,128]{1,0:T(2,128)S(1)}, f32[2,128]{1,0:T(2,128)S(1)}, u32[]{:S(2)}, u32[]{:S(2)}) collective-permute-start(f32[2,128]{1,0:T(2,128)S(1)} %add.12), channel_id=1, source_target_pairs={{0,128},{32,160},{64,192},{96,224},{128,0},{160,32},{192,64},{224,... | collective-permute-start | bytes 3080 | tf_op jit(solution)/shard_map/ppermute | solution.py:611
  49.9 3.6 %collective-permute-start.1 = (f32[2,128]{1,0:T(2,128)S(1)}, f32[2,128]{1,0:T(2,128)S(1)}, u32[]{:S(2)}, u32[]{:S(2)}) collective-permute-start(f32[2,128]{1,0:T(2,128)S(1)} %add.12), channel_id=1, source_target_pairs={{0,64},{32,96},{64,0},{96,32},{128,192},{160,224},{192,128},{224,1... | collective-permute-start | bytes 3080 | tf_op jit(solution)/shard_map/ppermute | solution.py:611

commit v6 on v5

--- a/solution.py
+++ b/solution.py
@@ -164,12 +164,26 @@
     return [rhs[v] * inverse(slack[v]) for v in everyone]
 
 
+PITCH = 17
+
+
+def store_turned(target, v, block):
+    for n in range(16):
+        target[pl.ds(v * 8 * PITCH + n // 2 * PITCH + n % 2 * 8, 8), :] = block[8 * n : 8 * n + 8, :]
+
+
+def load_turned(source, v):
+    return jnp.concatenate(
+        [source[pl.ds(v * 8 * PITCH + n // 2 * PITCH + n % 2 * 8, 8), :] for n in range(16)], axis=0
+    )
+
+
 def solve_rows(turned, faces, leak, rate, wind, hold_a, hold_b, hold_c, rows):
     everyone = range(8)
     depth = 16
 
     def at(v, i):
-        return pl.ds(v * 128 + i, 8, stride=depth)
+        return pl.ds(v * 8 * PITCH + i, 8, stride=PITCH)
 
     def keep(i, v):
         return pl.ds((i * 8 + v) * 8, 8)
@@ -316,7 +330,7 @@
                 (2 * h + 1, jnp.where(low, other, face)),
             ):
                 tile = jnp.concatenate([item] * 16, axis=0)
-                faces[pl.ds((f * 4 + yb) * 128, 128), :] = tile.T
+                store_turned(faces, f * 4 + yb, tile.T)
         start = jnp.broadcast_to(upper[:, 0:1], (8, 128))
         start = jnp.where(rows == lanes % 4, start, 0.0)
         start = jnp.broadcast_to(jnp.sum(start, axis=0, keepdims=True), (8, 128))
@@ -361,12 +375,10 @@
 
     solve_levels(cot, surf, scale, table, levels, hold_a, hold_c, low, halves)
     for v in range(8):
-        block = pl.ds(v * 128, 128)
-        turned[block, :] = levels[block, :].T
+        store_turned(turned, v, levels[pl.ds(v * 128, 128), :].T)
     solve_rows(turned, faces, leak, rate_y, wind_y, hold_a, hold_b, hold_c, rows)
     for v in range(8):
-        block = pl.ds(v * 128, 128)
-        levels[block, :] = turned[block, :].T
+        levels[pl.ds(v * 128, 128), :] = load_turned(turned, v).T
 
     for v in range(8):
         line = [surf_rows[pl.ds(v * 4 + x, 1), :] for x in range(4)]
@@ -574,7 +586,9 @@
         out_specs=(vmem,) * 4,
         scratch_shapes=[pltpu.SMEM(item.shape, item.dtype) for item in small]
         + [pltpu.VMEM(item.shape, item.dtype) for item in (classes, cells)]
-        + [pltpu.VMEM((1024, 128), F32)] * 7
+        + [pltpu.VMEM((1024, 128), F32)] * 2
+        + [pltpu.VMEM((64 * PITCH, 128), F32)] * 2
+        + [pltpu.VMEM((1024, 128), F32)] * 3
         + [pltpu.VMEM((32, 128), F32), pltpu.SemaphoreType.DMA((9,))],
         compiler_params=params,
     )(*(pltpu.with_memory_space_constraint(item, pltpu.HBM) for item in operands))

time: 54.3 us -> 54 us (level)
  no operation moved by 1% of the time
where the time goes in v6:
time: 54 us; the launch traced here: 53.9 us
  blocking collectives  38.1 us (71%)
  starting transfers between devices  7.08 us (13%)
  Pallas kernels  4.13 us (8%)
  waiting for transfers between devices  3.27 us (6%)
  between operations  0.66 us (1%)
  other arithmetic  0.57 us (1%)
    all_to_all x1, blocking collectives, on_device(): lax.all_to_all(sent.reshape(slabs, SEND, 1, 128), 'tile', 0, 0)  23.5 us
    all_to_all x1, blocking collectives, on_device(): ends = lax.all_to_all(ends, 'tile', 0, 0)  14.7 us
    ppermute x1, starting transfers between devices, on_device(): lax.ppermute(grad, 'scen', [(i, i ^ 1) for i in range(groups)])  3.76 us
    ppermute x3, starting transfers between devices, on_device(): lax.ppermute(grad, 'scen', [(i, i ^ step) for i in range(groups)])  3.31 us
    pallas_call x1, Pallas kernels, on_device(): pl.pallas_call(first_kernel, out_shape=(jax.ShapeDtypeStruct((slabs * SEN...  2.46 us
    ppermute x3, waiting for transfers between devices, on_device(): lax.ppermute(grad, 'scen', [(i, i ^ step) for i in range(groups)])  2.45 us
  transfers between devices with their start and end apart: 4, of which 2 were waited for; matrix products, arithmetic and copies ran while one was open for 0% of the time, Pallas kernels for 2%

profile of v6, /device:TPU:1, one launch (start us, length us, event | category | flops | bytes accessed | tf_op | source)
XLA Modules:
  0.0 53.9 jit_solution(11179676005904912876)
XLA Ops:
  0.6 2.5 %shard_map.95 = (f32[544,128]{1,0:T(8,128)S(1)}, f32[32,48,128]{2,1,0:T(8,128)S(1)}, f32[13,8,128]{2,1,0:T(8,128)S(1)}, bf16[512,128]{1,0:T(8,128)(2,1)S(1)}) custom-call(s32[4]{0:T(128)} %ids_in.1, f32[8,64]{1,0:T(8,128)} %bitcast.25, f32[2,17]{1,0:T(2,128)} %class_diff_in.1, f32[8]{0:T(128)} %scale_in.1, f32[8]{0:T(128)} %emit_in.1, s32[16,128]{1,0:T(8,128)} %bitcast.23, ...), custom_call_target="tpu_custom_call" | custom-call | tf_op jit(solution)/shard_map/pallas_call | solution.py:577
  3.1 23.5 %all_to_all.10 = f32[32,17,1,128]{3,2,1,0:T(1,128)S(1)} all-to-all(f32[32,17,1,128]{3,2,1,0:T(1,128)S(1)} %bitcast.20), channel_id=1, replica_groups=mesh['scen'=8,'tile'=32] {'tile'}, dimensions={0} | all-to-all | bytes 557056 | tf_op jit(solution)/shard_map/all_to_all | solution.py:595
  26.6 0.5 shard_map.96
  27.1 14.7 %all_to_all.11.ends = f32[32,16,128]{2,1,0:T(8,128)S(1)} all-to-all(f32[32,16,128]{2,1,0:T(8,128)S(1)} %shard_map.96), channel_id=1, replica_groups=mesh['scen'=8,'tile'=32] {'tile'}, dimensions={0} | all-to-all | bytes 524288 | tf_op jit(solution)/shard_map/all_to_all | solution.py:604
  41.8 0.3 shard_map.97
  42.0 3.8 %collective-permute-start = (f32[2,128]{1,0:T(2,128)S(1)}, f32[2,128]{1,0:T(2,128)S(1)}, u32[]{:S(2)}, u32[]{:S(2)}) collective-permute-start(f32[2,128]{1,0:T(2,128)S(1)} %get-tuple-element.13), channel_id=1, source_target_pairs={{0,32},{32,0},{64,96},{96,64},{128,160},{160,128},{192,224},{224,1... | collective-permute-start | bytes 3080 | tf_op jit(solution)/shard_map/ppermute | solution.py:623
  45.8 0.8 %collective-permute-done = f32[2,128]{1,0:T(2,128)S(1)} collective-permute-done((f32[2,128]{1,0:T(2,128)S(1)}, f32[2,128]{1,0:T(2,128)S(1)}, u32[]{:S(2)}, u32[]{:S(2)}) %collective-permute-start) | collective-permute-done | bytes 1056 | tf_op jit(solution)/shard_map/ppermute | solution.py:623
  46.6 2.7 %collective-permute-start.3 = (f32[2,128]{1,0:T(2,128)S(1)}, f32[2,128]{1,0:T(2,128)S(1)}, u32[]{:S(2)}, u32[]{:S(2)}) collective-permute-start(f32[2,128]{1,0:T(2,128)S(1)} %add.12), channel_id=1, source_target_pairs={{0,192},{32,224},{64,128},{96,160},{128,64},{160,96},{192,0},{224,... | collective-permute-start | bytes 3080 | tf_op jit(solution)/shard_map/ppermute | solution.py:625
  49.4 0.3 collective-permute-start.2
  49.7 0.2 collective-permute-start.1
  49.9 0.9 %shard_map.98 = f32[1024,128]{1,0:T(8,128)} custom-call(f32[32,16,128]{2,1,0:T(8,128)S(1)} %get-tuple-element.12.ends, f32[32,48,128]{2,1,0:T(8,128)S(1)} %get-tuple-element.11.kept), custom_call_target="tpu_custom_call" | custom-call | tf_op jit(solution)/shard_map/pallas_call | solution.py:615
  50.8 0.0 collective-permute-done.3
  50.8 2.4 %collective-permute-done.2 = f32[2,128]{1,0:T(2,128)S(1)} collective-permute-done((f32[2,128]{1,0:T(2,128)S(1)}, f32[2,128]{1,0:T(2,128)S(1)}, u32[]{:S(2)}, u32[]{:S(2)}) %collective-permute-start.2) | collective-permute-done | bytes 1056 | tf_op jit(solution)/shard_map/ppermute | solution.py:625
  53.3 0.0 collective-permute-done.1
  53.3 0.6 %add_add_fusion = f32[2,128]{1,0:T(2,128)} fusion(f32[2,128]{1,0:T(2,128)S(1)} %collective-permute-done.2, f32[2,128]{1,0:T(2,128)S(1)} %collective-permute-done.3, f32[2,128]{1,0:T(2,128)S(1)} %add.12, f32[2,128]{1,0:T(2,128)S(1)} %collective-permute-done.1), kind=kLoop, calls=%fused_computation | loop fusion | flops 768 | bytes 5120 | tf_op jit(solution)/shard_map/add | solution.py:627
  (1 shorter events, 0.0 us)
Async XLA Ops:
  42.0 4.6 %collective-permute-start = (f32[2,128]{1,0:T(2,128)S(1)}, f32[2,128]{1,0:T(2,128)S(1)}, u32[]{:S(2)}, u32[]{:S(2)}) collective-permute-start(f32[2,128]{1,0:T(2,128)S(1)} %get-tuple-element.13), channel_id=1, source_target_pairs={{0,32},{32,0},{64,96},{96,64},{128,160},{160,128},{192,224},{224,1... | collective-permute-start | bytes 3080 | tf_op jit(solution)/shard_map/ppermute | solution.py:623
  46.6 4.2 %collective-permute-start.3 = (f32[2,128]{1,0:T(2,128)S(1)}, f32[2,128]{1,0:T(2,128)S(1)}, u32[]{:S(2)}, u32[]{:S(2)}) collective-permute-start(f32[2,128]{1,0:T(2,128)S(1)} %add.12), channel_id=1, source_target_pairs={{0,192},{32,224},{64,128},{96,160},{128,64},{160,96},{192,0},{224,... | collective-permute-start | bytes 3080 | tf_op jit(solution)/shard_map/ppermute | solution.py:625
  49.4 3.9 %collective-permute-start.2 = (f32[2,128]{1,0:T(2,128)S(1)}, f32[2,128]{1,0:T(2,128)S(1)}, u32[]{:S(2)}, u32[]{:S(2)}) collective-permute-start(f32[2,128]{1,0:T(2,128)S(1)} %add.12), channel_id=1, source_target_pairs={{0,128},{32,160},{64,192},{96,224},{128,0},{160,32},{192,64},{224,... | collective-permute-start | bytes 3080 | tf_op jit(solution)/shard_map/ppermute | solution.py:625
  49.7 3.6 %collective-permute-start.1 = (f32[2,128]{1,0:T(2,128)S(1)}, f32[2,128]{1,0:T(2,128)S(1)}, u32[]{:S(2)}, u32[]{:S(2)}) collective-permute-start(f32[2,128]{1,0:T(2,128)S(1)} %add.12), channel_id=1, source_target_pairs={{0,64},{32,96},{64,0},{96,32},{128,192},{160,224},{192,128},{224,1... | collective-permute-start | bytes 3080 | tf_op jit(solution)/shard_map/ppermute | solution.py:625

commit v7 on v6

--- a/solution.py
+++ b/solution.py
@@ -405,23 +405,25 @@
     groups = lane() // 32
     slabs = ends.shape[0]
     strip = lax.axis_index("tile") % 4
+    lasts = []
+    spread[pl.ds(5 * slabs, 8), :] = jnp.zeros((8, 128), F32)
     for q in range(slabs // 8):
         shared = got[pl.ds(q * 8 * SEND + 16, 8, stride=SEND), :]
         turned = [pltpu.roll(shared, 32 * d, axis=1) if d else shared for d in range(4)]
-        for x in range(4):
-            spread[pl.ds(x * slabs + q * 8, 8), :] = pick(
-                groups, [turned[(p - x) % 4] for p in range(4)]
-            )
+        line = [pick(groups, [turned[(p - x) % 4] for p in range(4)]) for x in range(4)]
+        for x in range(3):
+            spread[pl.ds(x * slabs + q * 8, 8), :] = (line[x] + line[x + 1]) * 0.5
+        spread[pl.ds(4 * slabs + q * 8, 8), :] = line[0]
+        lasts.append(line[3])
+    for q in range(slabs // 8):
+        onward = spread[pl.ds(4 * slabs + q * 8 + 1, 8), :]
+        spread[pl.ds(3 * slabs + q * 8, 8), :] = (lasts[q] + onward) * 0.5
     rate = vectors[strip]
     wind = vectors[4]
     below, above, slack, rhs = [], [], [], []
-    line = None
-    outer = None
+    outer = rate * (spread[pl.ds(4 * slabs, 1), :] * 0.5)
     for k in range(slabs):
-        line = [spread[pl.ds(x * slabs + k, 1), :] for x in range(4)]
-        if k == 0:
-            outer = rate * (line[0] * 0.5)
-        e01, e12, e23 = (rate * ((line[x] + line[x + 1]) * 0.5) for x in range(3))
+        e01, e12, e23 = (rate * spread[pl.ds(x * slabs + k, 1), :] for x in range(3))
         one_inv, one_fill, one_upper, two_inv, two_fill, two_slack, two_next = inner_coefs(
             e01, e12, e23, wind
         )
@@ -436,10 +438,7 @@
         above.append(q0 * (one_upper * (two_next * two_inv)))
         slack.append(own)
         rhs.append(got[pl.ds(k * SEND, 8), :])
-        if k < slabs - 1:
-            outer = rate * ((line[3] + spread[pl.ds(k + 1, 1), :]) * 0.5)
-        else:
-            outer = rate * (line[3] * 0.5)
+        outer = rate * spread[pl.ds(3 * slabs + k, 1), :]
         own = 1.0 + e23 * two_slack
         below.append(e23 * (two_fill * two_inv))
         if k < slabs - 1:
@@ -598,7 +597,7 @@
         out_shape=jax.ShapeDtypeStruct((slabs, 16, 128), F32),
         in_specs=[vmem] * 2,
         out_specs=vmem,
-        scratch_shapes=[pltpu.VMEM((4 * slabs, 128), F32)],
+        scratch_shapes=[pltpu.VMEM((5 * slabs + 8, 128), F32)],
         compiler_params=params,
     )(vectors, got)
     ends = lax.all_to_all(ends, "tile", 0, 0)

time: 54 us -> 54 us (level)
  no operation moved by 1% of the time
where the time goes in v7:
time: 54 us; the launch traced here: 53.8 us
  blocking collectives  38.1 us (71%)
  starting transfers between devices  7.08 us (13%)
  Pallas kernels  4.09 us (8%)
  waiting for transfers between devices  3.27 us (6%)
  between operations  0.66 us (1%)
  other arithmetic  0.57 us (1%)
    all_to_all x1, blocking collectives, on_device(): lax.all_to_all(sent.reshape(slabs, SEND, 1, 128), 'tile', 0, 0)  23.5 us
    all_to_all x1, blocking collectives, on_device(): ends = lax.all_to_all(ends, 'tile', 0, 0)  14.7 us
    ppermute x1, starting transfers between devices, on_device(): lax.ppermute(grad, 'scen', [(i, i ^ 1) for i in range(groups)])  3.76 us
    ppermute x3, starting transfers between devices, on_device(): lax.ppermute(grad, 'scen', [(i, i ^ step) for i in range(groups)])  3.31 us
    pallas_call x1, Pallas kernels, on_device(): pl.pallas_call(first_kernel, out_shape=(jax.ShapeDtypeStruct((slabs * SEN...  2.46 us
    ppermute x3, waiting for transfers between devices, on_device(): lax.ppermute(grad, 'scen', [(i, i ^ step) for i in range(groups)])  2.45 us
  transfers between devices with their start and end apart: 4, of which 2 were waited for; matrix products, arithmetic and copies ran while one was open for 0% of the time, Pallas kernels for 2%

profile of v7, /device:TPU:1, one launch (start us, length us, event | category | flops | bytes accessed | tf_op | source)
XLA Modules:
  0.0 53.8 jit_solution(8219815612393475852)
XLA Ops:
  0.6 2.5 %shard_map.95 = (f32[544,128]{1,0:T(8,128)S(1)}, f32[32,48,128]{2,1,0:T(8,128)S(1)}, f32[13,8,128]{2,1,0:T(8,128)S(1)}, bf16[512,128]{1,0:T(8,128)(2,1)S(1)}) custom-call(s32[4]{0:T(128)} %ids_in.1, f32[8,64]{1,0:T(8,128)} %bitcast.25, f32[2,17]{1,0:T(2,128)} %class_diff_in.1, f32[8]{0:T(128)} %scale_in.1, f32[8]{0:T(128)} %emit_in.1, s32[16,128]{1,0:T(8,128)} %bitcast.23, ...), custom_call_target="tpu_custom_call" | custom-call | tf_op jit(solution)/shard_map/pallas_call | solution.py:576
  3.1 23.5 %all_to_all.10 = f32[32,17,1,128]{3,2,1,0:T(1,128)S(1)} all-to-all(f32[32,17,1,128]{3,2,1,0:T(1,128)S(1)} %bitcast.20), channel_id=1, replica_groups=mesh['scen'=8,'tile'=32] {'tile'}, dimensions={0} | all-to-all | bytes 557056 | tf_op jit(solution)/shard_map/all_to_all | solution.py:594
  26.6 0.5 shard_map.96
  27.0 14.7 %all_to_all.11.ends = f32[32,16,128]{2,1,0:T(8,128)S(1)} all-to-all(f32[32,16,128]{2,1,0:T(8,128)S(1)} %shard_map.96), channel_id=1, replica_groups=mesh['scen'=8,'tile'=32] {'tile'}, dimensions={0} | all-to-all | bytes 524288 | tf_op jit(solution)/shard_map/all_to_all | solution.py:603
  41.7 0.3 shard_map.97
  42.0 3.8 %collective-permute-start = (f32[2,128]{1,0:T(2,128)S(1)}, f32[2,128]{1,0:T(2,128)S(1)}, u32[]{:S(2)}, u32[]{:S(2)}) collective-permute-start(f32[2,128]{1,0:T(2,128)S(1)} %get-tuple-element.13), channel_id=1, source_target_pairs={{0,32},{32,0},{64,96},{96,64},{128,160},{160,128},{192,224},{224,1... | collective-permute-start | bytes 3080 | tf_op jit(solution)/shard_map/ppermute | solution.py:622
  45.8 0.8 %collective-permute-done = f32[2,128]{1,0:T(2,128)S(1)} collective-permute-done((f32[2,128]{1,0:T(2,128)S(1)}, f32[2,128]{1,0:T(2,128)S(1)}, u32[]{:S(2)}, u32[]{:S(2)}) %collective-permute-start) | collective-permute-done | bytes 1056 | tf_op jit(solution)/shard_map/ppermute | solution.py:622
  46.6 2.7 %collective-permute-start.3 = (f32[2,128]{1,0:T(2,128)S(1)}, f32[2,128]{1,0:T(2,128)S(1)}, u32[]{:S(2)}, u32[]{:S(2)}) collective-permute-start(f32[2,128]{1,0:T(2,128)S(1)} %add.12), channel_id=1, source_target_pairs={{0,192},{32,224},{64,128},{96,160},{128,64},{160,96},{192,0},{224,... | collective-permute-start | bytes 3080 | tf_op jit(solution)/shard_map/ppermute | solution.py:624
  49.3 0.3 collective-permute-start.2
  49.7 0.2 collective-permute-start.1
  49.9 0.9 %shard_map.98 = f32[1024,128]{1,0:T(8,128)} custom-call(f32[32,16,128]{2,1,0:T(8,128)S(1)} %get-tuple-element.12.ends, f32[32,48,128]{2,1,0:T(8,128)S(1)} %get-tuple-element.11.kept), custom_call_target="tpu_custom_call" | custom-call | tf_op jit(solution)/shard_map/pallas_call | solution.py:614
  50.8 0.0 collective-permute-done.3
  50.8 2.4 %collective-permute-done.2 = f32[2,128]{1,0:T(2,128)S(1)} collective-permute-done((f32[2,128]{1,0:T(2,128)S(1)}, f32[2,128]{1,0:T(2,128)S(1)}, u32[]{:S(2)}, u32[]{:S(2)}) %collective-permute-start.2) | collective-permute-done | bytes 1056 | tf_op jit(solution)/shard_map/ppermute | solution.py:624
  53.2 0.0 collective-permute-done.1
  53.2 0.6 %add_add_fusion = f32[2,128]{1,0:T(2,128)} fusion(f32[2,128]{1,0:T(2,128)S(1)} %collective-permute-done.2, f32[2,128]{1,0:T(2,128)S(1)} %collective-permute-done.3, f32[2,128]{1,0:T(2,128)S(1)} %add.12, f32[2,128]{1,0:T(2,128)S(1)} %collective-permute-done.1), kind=kLoop, calls=%fused_computation | loop fusion | flops 768 | bytes 5120 | tf_op jit(solution)/shard_map/add | solution.py:626
  (1 shorter events, 0.0 us)
Async XLA Ops:
  42.0 4.6 %collective-permute-start = (f32[2,128]{1,0:T(2,128)S(1)}, f32[2,128]{1,0:T(2,128)S(1)}, u32[]{:S(2)}, u32[]{:S(2)}) collective-permute-start(f32[2,128]{1,0:T(2,128)S(1)} %get-tuple-element.13), channel_id=1, source_target_pairs={{0,32},{32,0},{64,96},{96,64},{128,160},{160,128},{192,224},{224,1... | collective-permute-start | bytes 3080 | tf_op jit(solution)/shard_map/ppermute | solution.py:622
  46.6 4.2 %collective-permute-start.3 = (f32[2,128]{1,0:T(2,128)S(1)}, f32[2,128]{1,0:T(2,128)S(1)}, u32[]{:S(2)}, u32[]{:S(2)}) collective-permute-start(f32[2,128]{1,0:T(2,128)S(1)} %add.12), channel_id=1, source_target_pairs={{0,192},{32,224},{64,128},{96,160},{128,64},{160,96},{192,0},{224,... | collective-permute-start | bytes 3080 | tf_op jit(solution)/shard_map/ppermute | solution.py:624
  49.3 3.9 %collective-permute-start.2 = (f32[2,128]{1,0:T(2,128)S(1)}, f32[2,128]{1,0:T(2,128)S(1)}, u32[]{:S(2)}, u32[]{:S(2)}) collective-permute-start(f32[2,128]{1,0:T(2,128)S(1)} %add.12), channel_id=1, source_target_pairs={{0,128},{32,160},{64,192},{96,224},{128,0},{160,32},{192,64},{224,... | collective-permute-start | bytes 3080 | tf_op jit(solution)/shard_map/ppermute | solution.py:624
  49.7 3.6 %collective-permute-start.1 = (f32[2,128]{1,0:T(2,128)S(1)}, f32[2,128]{1,0:T(2,128)S(1)}, u32[]{:S(2)}, u32[]{:S(2)}) collective-permute-start(f32[2,128]{1,0:T(2,128)S(1)} %add.12), channel_id=1, source_target_pairs={{0,64},{32,96},{64,0},{96,32},{128,192},{160,224},{192,128},{224,1... | collective-permute-start | bytes 3080 | tf_op jit(solution)/shard_map/ppermute | solution.py:624

commit v8 on v6

--- a/solution.py
+++ b/solution.py
@@ -622,7 +622,7 @@
     )(ends, kept)
     grad = grad + lax.ppermute(grad, "scen", [(i, i ^ 1) for i in range(groups)])
     shifted = [
-        lax.ppermute(grad, "scen", [(i, i ^ step) for i in range(groups)]) for step in (2, 4, 6)
+        lax.ppermute(grad, "scen", [(i, i ^ step) for i in range(groups)]) for step in (2, 6, 4)
     ]
     grad = (grad + shifted[0]) + (shifted[1] + shifted[2])
     state = state.reshape(4, 2, 8, 4, 4, 128).transpose(0, 1, 2, 4, 3, 5).reshape(cotangent.shape)

time: 54 us -> 53.9 us (level)
  no operation moved by 1% of the time
where the time goes in v8:
time: 53.9 us; the launch traced here: 53.7 us
  blocking collectives  38.1 us (71%)
  starting transfers between devices  7.46 us (14%)
  Pallas kernels  4.13 us (8%)
  waiting for transfers between devices  2.78 us (5%)
  between operations  0.66 us (1%)
  other arithmetic  0.57 us (1%)
    all_to_all x1, blocking collectives, on_device(): lax.all_to_all(sent.reshape(slabs, SEND, 1, 128), 'tile', 0, 0)  23.5 us
    all_to_all x1, blocking collectives, on_device(): ends = lax.all_to_all(ends, 'tile', 0, 0)  14.7 us
    ppermute x1, starting transfers between devices, on_device(): lax.ppermute(grad, 'scen', [(i, i ^ 1) for i in range(groups)])  3.76 us
    ppermute x3, starting transfers between devices, on_device(): lax.ppermute(grad, 'scen', [(i, i ^ step) for i in range(groups)])  3.69 us
    pallas_call x1, Pallas kernels, on_device(): pl.pallas_call(first_kernel, out_shape=(jax.ShapeDtypeStruct((slabs * SEN...  2.46 us
    ppermute x3, waiting for transfers between devices, on_device(): lax.ppermute(grad, 'scen', [(i, i ^ step) for i in range(groups)])  1.96 us
  transfers between devices with their start and end apart: 4, of which 2 were waited for; matrix products, arithmetic and copies ran while one was open for 0% of the time, Pallas kernels for 2%

profile of v8, /device:TPU:1, one launch (start us, length us, event | category | flops | bytes accessed | tf_op | source)
XLA Modules:
  0.0 53.7 jit_solution(13274284697218660862)
XLA Ops:
  0.6 2.5 %shard_map.95 = (f32[544,128]{1,0:T(8,128)S(1)}, f32[32,48,128]{2,1,0:T(8,128)S(1)}, f32[13,8,128]{2,1,0:T(8,128)S(1)}, bf16[512,128]{1,0:T(8,128)(2,1)S(1)}) custom-call(s32[4]{0:T(128)} %ids_in.1, f32[8,64]{1,0:T(8,128)} %bitcast.25, f32[2,17]{1,0:T(2,128)} %class_diff_in.1, f32[8]{0:T(128)} %scale_in.1, f32[8]{0:T(128)} %emit_in.1, s32[16,128]{1,0:T(8,128)} %bitcast.23, ...), custom_call_target="tpu_custom_call" | custom-call | tf_op jit(solution)/shard_map/pallas_call | solution.py:577
  3.1 23.5 %all_to_all.10 = f32[32,17,1,128]{3,2,1,0:T(1,128)S(1)} all-to-all(f32[32,17,1,128]{3,2,1,0:T(1,128)S(1)} %bitcast.20), channel_id=1, replica_groups=mesh['scen'=8,'tile'=32] {'tile'}, dimensions={0} | all-to-all | bytes 557056 | tf_op jit(solution)/shard_map/all_to_all | solution.py:595
  26.6 0.5 shard_map.96
  27.1 14.7 %all_to_all.11.ends = f32[32,16,128]{2,1,0:T(8,128)S(1)} all-to-all(f32[32,16,128]{2,1,0:T(8,128)S(1)} %shard_map.96), channel_id=1, replica_groups=mesh['scen'=8,'tile'=32] {'tile'}, dimensions={0} | all-to-all | bytes 524288 | tf_op jit(solution)/shard_map/all_to_all | solution.py:604
  41.8 0.3 shard_map.97
  42.0 3.8 %collective-permute-start = (f32[2,128]{1,0:T(2,128)S(1)}, f32[2,128]{1,0:T(2,128)S(1)}, u32[]{:S(2)}, u32[]{:S(2)}) collective-permute-start(f32[2,128]{1,0:T(2,128)S(1)} %get-tuple-element.13), channel_id=1, source_target_pairs={{0,32},{32,0},{64,96},{96,64},{128,160},{160,128},{192,224},{224,1... | collective-permute-start | bytes 3080 | tf_op jit(solution)/shard_map/ppermute | solution.py:623
  45.8 0.8 %collective-permute-done = f32[2,128]{1,0:T(2,128)S(1)} collective-permute-done((f32[2,128]{1,0:T(2,128)S(1)}, f32[2,128]{1,0:T(2,128)S(1)}, u32[]{:S(2)}, u32[]{:S(2)}) %collective-permute-start) | collective-permute-done | bytes 1056 | tf_op jit(solution)/shard_map/ppermute | solution.py:623
  46.6 2.9 %collective-permute-start.3 = (f32[2,128]{1,0:T(2,128)S(1)}, f32[2,128]{1,0:T(2,128)S(1)}, u32[]{:S(2)}, u32[]{:S(2)}) collective-permute-start(f32[2,128]{1,0:T(2,128)S(1)} %add.12), channel_id=1, source_target_pairs={{0,128},{32,160},{64,192},{96,224},{128,0},{160,32},{192,64},{224,... | collective-permute-start | bytes 3080 | tf_op jit(solution)/shard_map/ppermute | solution.py:625
  49.5 0.8 %collective-permute-start.2 = (f32[2,128]{1,0:T(2,128)S(1)}, f32[2,128]{1,0:T(2,128)S(1)}, u32[]{:S(2)}, u32[]{:S(2)}) collective-permute-start(f32[2,128]{1,0:T(2,128)S(1)} %add.12), channel_id=1, source_target_pairs={{0,192},{32,224},{64,128},{96,160},{128,64},{160,96},{192,0},{224,... | collective-permute-start | bytes 3080 | tf_op jit(solution)/shard_map/ppermute | solution.py:625
  50.3 0.0 collective-permute-start.1
  50.3 0.9 %shard_map.98 = f32[1024,128]{1,0:T(8,128)} custom-call(f32[32,16,128]{2,1,0:T(8,128)S(1)} %get-tuple-element.12.ends, f32[32,48,128]{2,1,0:T(8,128)S(1)} %get-tuple-element.11.kept), custom_call_target="tpu_custom_call" | custom-call | tf_op jit(solution)/shard_map/pallas_call | solution.py:615
  51.2 0.0 collective-permute-done.3
  51.2 2.0 %collective-permute-done.2 = f32[2,128]{1,0:T(2,128)S(1)} collective-permute-done((f32[2,128]{1,0:T(2,128)S(1)}, f32[2,128]{1,0:T(2,128)S(1)}, u32[]{:S(2)}, u32[]{:S(2)}) %collective-permute-start.2) | collective-permute-done | bytes 1056 | tf_op jit(solution)/shard_map/ppermute | solution.py:625
  53.2 0.0 collective-permute-done.1
  53.2 0.6 %add_add_fusion = f32[2,128]{1,0:T(2,128)} fusion(f32[2,128]{1,0:T(2,128)S(1)} %collective-permute-done.2, f32[2,128]{1,0:T(2,128)S(1)} %collective-permute-done.3, f32[2,128]{1,0:T(2,128)S(1)} %add.12, f32[2,128]{1,0:T(2,128)S(1)} %collective-permute-done.1), kind=kLoop, calls=%fused_computation | loop fusion | flops 768 | bytes 5120 | tf_op jit(solution)/shard_map/add | solution.py:627
  (1 shorter events, 0.0 us)
Async XLA Ops:
  42.0 4.6 %collective-permute-start = (f32[2,128]{1,0:T(2,128)S(1)}, f32[2,128]{1,0:T(2,128)S(1)}, u32[]{:S(2)}, u32[]{:S(2)}) collective-permute-start(f32[2,128]{1,0:T(2,128)S(1)} %get-tuple-element.13), channel_id=1, source_target_pairs={{0,32},{32,0},{64,96},{96,64},{128,160},{160,128},{192,224},{224,1... | collective-permute-start | bytes 3080 | tf_op jit(solution)/shard_map/ppermute | solution.py:623
  46.6 4.6 %collective-permute-start.3 = (f32[2,128]{1,0:T(2,128)S(1)}, f32[2,128]{1,0:T(2,128)S(1)}, u32[]{:S(2)}, u32[]{:S(2)}) collective-permute-start(f32[2,128]{1,0:T(2,128)S(1)} %add.12), channel_id=1, source_target_pairs={{0,128},{32,160},{64,192},{96,224},{128,0},{160,32},{192,64},{224,... | collective-permute-start | bytes 3080 | tf_op jit(solution)/shard_map/ppermute | solution.py:625
  49.5 3.6 %collective-permute-start.2 = (f32[2,128]{1,0:T(2,128)S(1)}, f32[2,128]{1,0:T(2,128)S(1)}, u32[]{:S(2)}, u32[]{:S(2)}) collective-permute-start(f32[2,128]{1,0:T(2,128)S(1)} %add.12), channel_id=1, source_target_pairs={{0,192},{32,224},{64,128},{96,160},{128,64},{160,96},{192,0},{224,... | collective-permute-start | bytes 3080 | tf_op jit(solution)/shard_map/ppermute | solution.py:625
  50.3 2.9 %collective-permute-start.1 = (f32[2,128]{1,0:T(2,128)S(1)}, f32[2,128]{1,0:T(2,128)S(1)}, u32[]{:S(2)}, u32[]{:S(2)}) collective-permute-start(f32[2,128]{1,0:T(2,128)S(1)} %add.12), channel_id=1, source_target_pairs={{0,64},{32,96},{64,0},{96,32},{128,192},{160,224},{192,128},{224,1... | collective-permute-start | bytes 3080 | tf_op jit(solution)/shard_map/ppermute | solution.py:625

commit v9 on v7

--- a/solution.py
+++ b/solution.py
@@ -621,7 +621,7 @@
     )(ends, kept)
     grad = grad + lax.ppermute(grad, "scen", [(i, i ^ 1) for i in range(groups)])
     shifted = [
-        lax.ppermute(grad, "scen", [(i, i ^ step) for i in range(groups)]) for step in (2, 4, 6)
+        lax.ppermute(grad, "scen", [(i, i ^ step) for i in range(groups)]) for step in (2, 6, 4)
     ]
     grad = (grad + shifted[0]) + (shifted[1] + shifted[2])
     state = state.reshape(4, 2, 8, 4, 4, 128).transpose(0, 1, 2, 4, 3, 5).reshape(cotangent.shape)

time: 54 us -> 53.9 us (level)
  no operation moved by 1% of the time
where the time goes in v9:
time: 53.9 us; the launch traced here: 53.7 us
  blocking collectives  38.1 us (71%)
  starting transfers between devices  7.46 us (14%)
  Pallas kernels  4.09 us (8%)
  waiting for transfers between devices  2.78 us (5%)
  between operations  0.66 us (1%)
  other arithmetic  0.57 us (1%)
    all_to_all x1, blocking collectives, on_device(): lax.all_to_all(sent.reshape(slabs, SEND, 1, 128), 'tile', 0, 0)  23.5 us
    all_to_all x1, blocking collectives, on_device(): ends = lax.all_to_all(ends, 'tile', 0, 0)  14.7 us
    ppermute x1, starting transfers between devices, on_device(): lax.ppermute(grad, 'scen', [(i, i ^ 1) for i in range(groups)])  3.76 us
    ppermute x3, starting transfers between devices, on_device(): lax.ppermute(grad, 'scen', [(i, i ^ step) for i in range(groups)])  3.69 us
    pallas_call x1, Pallas kernels, on_device(): pl.pallas_call(first_kernel, out_shape=(jax.ShapeDtypeStruct((slabs * SEN...  2.46 us
    ppermute x3, waiting for transfers between devices, on_device(): lax.ppermute(grad, 'scen', [(i, i ^ step) for i in range(groups)])  1.96 us
  transfers between devices with their start and end apart: 4, of which 2 were waited for; matrix products, arithmetic and copies ran while one was open for 0% of the time, Pallas kernels for 2%

profile of v9, /device:TPU:1, one launch (start us, length us, event | category | flops | bytes accessed | tf_op | source)
XLA Modules:
  0.0 53.7 jit_solution(13992428580554475352)
XLA Ops:
  0.6 2.5 %shard_map.95 = (f32[544,128]{1,0:T(8,128)S(1)}, f32[32,48,128]{2,1,0:T(8,128)S(1)}, f32[13,8,128]{2,1,0:T(8,128)S(1)}, bf16[512,128]{1,0:T(8,128)(2,1)S(1)}) custom-call(s32[4]{0:T(128)} %ids_in.1, f32[8,64]{1,0:T(8,128)} %bitcast.25, f32[2,17]{1,0:T(2,128)} %class_diff_in.1, f32[8]{0:T(128)} %scale_in.1, f32[8]{0:T(128)} %emit_in.1, s32[16,128]{1,0:T(8,128)} %bitcast.23, ...), custom_call_target="tpu_custom_call" | custom-call | tf_op jit(solution)/shard_map/pallas_call | solution.py:576
  3.1 23.5 %all_to_all.10 = f32[32,17,1,128]{3,2,1,0:T(1,128)S(1)} all-to-all(f32[32,17,1,128]{3,2,1,0:T(1,128)S(1)} %bitcast.20), channel_id=1, replica_groups=mesh['scen'=8,'tile'=32] {'tile'}, dimensions={0} | all-to-all | bytes 557056 | tf_op jit(solution)/shard_map/all_to_all | solution.py:594
  26.6 0.5 shard_map.96
  27.0 14.7 %all_to_all.11.ends = f32[32,16,128]{2,1,0:T(8,128)S(1)} all-to-all(f32[32,16,128]{2,1,0:T(8,128)S(1)} %shard_map.96), channel_id=1, replica_groups=mesh['scen'=8,'tile'=32] {'tile'}, dimensions={0} | all-to-all | bytes 524288 | tf_op jit(solution)/shard_map/all_to_all | solution.py:603
  41.7 0.3 shard_map.97
  42.0 3.8 %collective-permute-start = (f32[2,128]{1,0:T(2,128)S(1)}, f32[2,128]{1,0:T(2,128)S(1)}, u32[]{:S(2)}, u32[]{:S(2)}) collective-permute-start(f32[2,128]{1,0:T(2,128)S(1)} %get-tuple-element.13), channel_id=1, source_target_pairs={{0,32},{32,0},{64,96},{96,64},{128,160},{160,128},{192,224},{224,1... | collective-permute-start | bytes 3080 | tf_op jit(solution)/shard_map/ppermute | solution.py:622
  45.8 0.8 %collective-permute-done = f32[2,128]{1,0:T(2,128)S(1)} collective-permute-done((f32[2,128]{1,0:T(2,128)S(1)}, f32[2,128]{1,0:T(2,128)S(1)}, u32[]{:S(2)}, u32[]{:S(2)}) %collective-permute-start) | collective-permute-done | bytes 1056 | tf_op jit(solution)/shard_map/ppermute | solution.py:622
  46.6 2.9 %collective-permute-start.3 = (f32[2,128]{1,0:T(2,128)S(1)}, f32[2,128]{1,0:T(2,128)S(1)}, u32[]{:S(2)}, u32[]{:S(2)}) collective-permute-start(f32[2,128]{1,0:T(2,128)S(1)} %add.12), channel_id=1, source_target_pairs={{0,128},{32,160},{64,192},{96,224},{128,0},{160,32},{192,64},{224,... | collective-permute-start | bytes 3080 | tf_op jit(solution)/shard_map/ppermute | solution.py:624
  49.5 0.8 %collective-permute-start.2 = (f32[2,128]{1,0:T(2,128)S(1)}, f32[2,128]{1,0:T(2,128)S(1)}, u32[]{:S(2)}, u32[]{:S(2)}) collective-permute-start(f32[2,128]{1,0:T(2,128)S(1)} %add.12), channel_id=1, source_target_pairs={{0,192},{32,224},{64,128},{96,160},{128,64},{160,96},{192,0},{224,... | collective-permute-start | bytes 3080 | tf_op jit(solution)/shard_map/ppermute | solution.py:624
  50.3 0.0 collective-permute-start.1
  50.3 0.9 %shard_map.98 = f32[1024,128]{1,0:T(8,128)} custom-call(f32[32,16,128]{2,1,0:T(8,128)S(1)} %get-tuple-element.12.ends, f32[32,48,128]{2,1,0:T(8,128)S(1)} %get-tuple-element.11.kept), custom_call_target="tpu_custom_call" | custom-call | tf_op jit(solution)/shard_map/pallas_call | solution.py:614
  51.2 0.0 collective-permute-done.3
  51.2 2.0 %collective-permute-done.2 = f32[2,128]{1,0:T(2,128)S(1)} collective-permute-done((f32[2,128]{1,0:T(2,128)S(1)}, f32[2,128]{1,0:T(2,128)S(1)}, u32[]{:S(2)}, u32[]{:S(2)}) %collective-permute-start.2) | collective-permute-done | bytes 1056 | tf_op jit(solution)/shard_map/ppermute | solution.py:624
  53.1 0.0 collective-permute-done.1
  53.1 0.6 %add_add_fusion = f32[2,128]{1,0:T(2,128)} fusion(f32[2,128]{1,0:T(2,128)S(1)} %collective-permute-done.2, f32[2,128]{1,0:T(2,128)S(1)} %collective-permute-done.3, f32[2,128]{1,0:T(2,128)S(1)} %add.12, f32[2,128]{1,0:T(2,128)S(1)} %collective-permute-done.1), kind=kLoop, calls=%fused_computation | loop fusion | flops 768 | bytes 5120 | tf_op jit(solution)/shard_map/add | solution.py:626
  (1 shorter events, 0.0 us)
Async XLA Ops:
  42.0 4.6 %collective-permute-start = (f32[2,128]{1,0:T(2,128)S(1)}, f32[2,128]{1,0:T(2,128)S(1)}, u32[]{:S(2)}, u32[]{:S(2)}) collective-permute-start(f32[2,128]{1,0:T(2,128)S(1)} %get-tuple-element.13), channel_id=1, source_target_pairs={{0,32},{32,0},{64,96},{96,64},{128,160},{160,128},{192,224},{224,1... | collective-permute-start | bytes 3080 | tf_op jit(solution)/shard_map/ppermute | solution.py:622
  46.6 4.6 %collective-permute-start.3 = (f32[2,128]{1,0:T(2,128)S(1)}, f32[2,128]{1,0:T(2,128)S(1)}, u32[]{:S(2)}, u32[]{:S(2)}) collective-permute-start(f32[2,128]{1,0:T(2,128)S(1)} %add.12), channel_id=1, source_target_pairs={{0,128},{32,160},{64,192},{96,224},{128,0},{160,32},{192,64},{224,... | collective-permute-start | bytes 3080 | tf_op jit(solution)/shard_map/ppermute | solution.py:624
  49.5 3.6 %collective-permute-start.2 = (f32[2,128]{1,0:T(2,128)S(1)}, f32[2,128]{1,0:T(2,128)S(1)}, u32[]{:S(2)}, u32[]{:S(2)}) collective-permute-start(f32[2,128]{1,0:T(2,128)S(1)} %add.12), channel_id=1, source_target_pairs={{0,192},{32,224},{64,128},{96,160},{128,64},{160,96},{192,0},{224,... | collective-permute-start | bytes 3080 | tf_op jit(solution)/shard_map/ppermute | solution.py:624
  50.3 2.9 %collective-permute-start.1 = (f32[2,128]{1,0:T(2,128)S(1)}, f32[2,128]{1,0:T(2,128)S(1)}, u32[]{:S(2)}, u32[]{:S(2)}) collective-permute-start(f32[2,128]{1,0:T(2,128)S(1)} %add.12), channel_id=1, source_target_pairs={{0,64},{32,96},{64,0},{96,32},{128,192},{160,224},{192,128},{224,1... | collective-permute-start | bytes 3080 | tf_op jit(solution)/shard_map/ppermute | solution.py:624

commit v10 on v8

--- a/solution.py
+++ b/solution.py
@@ -622,7 +622,7 @@
     )(ends, kept)
     grad = grad + lax.ppermute(grad, "scen", [(i, i ^ 1) for i in range(groups)])
     shifted = [
-        lax.ppermute(grad, "scen", [(i, i ^ step) for i in range(groups)]) for step in (2, 6, 4)
+        lax.ppermute(grad, "scen", [(i, i ^ step) for i in range(groups)]) for step in (6, 2, 4)
     ]
     grad = (grad + shifted[0]) + (shifted[1] + shifted[2])
     state = state.reshape(4, 2, 8, 4, 4, 128).transpose(0, 1, 2, 4, 3, 5).reshape(cotangent.shape)

time: 53.9 us -> 54.3 us (level)
  transfers between devices with their start and end apart: 4 -> 4, of which waited for: 2 -> 3; matrix products, arithmetic and copies ran while one was open for 0% -> 0% of each run, Pallas kernels for 2% -> 2%
where the time goes in v10:
time: 54.3 us; the launch traced here: 54.1 us
  blocking collectives  38.1 us (70%)
  starting transfers between devices  7.46 us (14%)
  Pallas kernels  4.13 us (8%)
  waiting for transfers between devices  3.18 us (6%)
  between operations  0.66 us (1%)
  other arithmetic  0.57 us (1%)
    all_to_all x1, blocking collectives, on_device(): lax.all_to_all(sent.reshape(slabs, SEND, 1, 128), 'tile', 0, 0)  23.5 us
    all_to_all x1, blocking collectives, on_device(): ends = lax.all_to_all(ends, 'tile', 0, 0)  14.7 us
    ppermute x1, starting transfers between devices, on_device(): lax.ppermute(grad, 'scen', [(i, i ^ 1) for i in range(groups)])  3.76 us
    ppermute x3, starting transfers between devices, on_device(): lax.ppermute(grad, 'scen', [(i, i ^ step) for i in range(groups)])  3.69 us
    pallas_call x1, Pallas kernels, on_device(): pl.pallas_call(first_kernel, out_shape=(jax.ShapeDtypeStruct((slabs * SEN...  2.46 us
    ppermute x3, waiting for transfers between devices, on_device(): lax.ppermute(grad, 'scen', [(i, i ^ step) for i in range(groups)])  2.36 us
  transfers between devices with their start and end apart: 4, of which 3 were waited for; matrix products, arithmetic and copies ran while one was open for 0% of the time, Pallas kernels for 2%

profile of v10, /device:TPU:1, one launch (start us, length us, event | category | flops | bytes accessed | tf_op | source)
XLA Modules:
  0.0 54.1 jit_solution(9561212045360831052)
XLA Ops:
  0.6 2.5 %shard_map.95 = (f32[544,128]{1,0:T(8,128)S(1)}, f32[32,48,128]{2,1,0:T(8,128)S(1)}, f32[13,8,128]{2,1,0:T(8,128)S(1)}, bf16[512,128]{1,0:T(8,128)(2,1)S(1)}) custom-call(s32[4]{0:T(128)} %ids_in.1, f32[8,64]{1,0:T(8,128)} %bitcast.25, f32[2,17]{1,0:T(2,128)} %class_diff_in.1, f32[8]{0:T(128)} %scale_in.1, f32[8]{0:T(128)} %emit_in.1, s32[16,128]{1,0:T(8,128)} %bitcast.23, ...), custom_call_target="tpu_custom_call" | custom-call | tf_op jit(solution)/shard_map/pallas_call | solution.py:577
  3.1 23.5 %all_to_all.10 = f32[32,17,1,128]{3,2,1,0:T(1,128)S(1)} all-to-all(f32[32,17,1,128]{3,2,1,0:T(1,128)S(1)} %bitcast.20), channel_id=1, replica_groups=mesh['scen'=8,'tile'=32] {'tile'}, dimensions={0} | all-to-all | bytes 557056 | tf_op jit(solution)/shard_map/all_to_all | solution.py:595
  26.6 0.5 shard_map.96
  27.1 14.7 %all_to_all.11.ends = f32[32,16,128]{2,1,0:T(8,128)S(1)} all-to-all(f32[32,16,128]{2,1,0:T(8,128)S(1)} %shard_map.96), channel_id=1, replica_groups=mesh['scen'=8,'tile'=32] {'tile'}, dimensions={0} | all-to-all | bytes 524288 | tf_op jit(solution)/shard_map/all_to_all | solution.py:604
  41.8 0.3 shard_map.97
  42.0 3.8 %collective-permute-start = (f32[2,128]{1,0:T(2,128)S(1)}, f32[2,128]{1,0:T(2,128)S(1)}, u32[]{:S(2)}, u32[]{:S(2)}) collective-permute-start(f32[2,128]{1,0:T(2,128)S(1)} %get-tuple-element.13), channel_id=1, source_target_pairs={{0,32},{32,0},{64,96},{96,64},{128,160},{160,128},{192,224},{224,1... | collective-permute-start | bytes 3080 | tf_op jit(solution)/shard_map/ppermute | solution.py:623
  45.8 0.8 %collective-permute-done = f32[2,128]{1,0:T(2,128)S(1)} collective-permute-done((f32[2,128]{1,0:T(2,128)S(1)}, f32[2,128]{1,0:T(2,128)S(1)}, u32[]{:S(2)}, u32[]{:S(2)}) %collective-permute-start) | collective-permute-done | bytes 1056 | tf_op jit(solution)/shard_map/ppermute | solution.py:623
  46.6 2.9 %collective-permute-start.3 = (f32[2,128]{1,0:T(2,128)S(1)}, f32[2,128]{1,0:T(2,128)S(1)}, u32[]{:S(2)}, u32[]{:S(2)}) collective-permute-start(f32[2,128]{1,0:T(2,128)S(1)} %add.12), channel_id=1, source_target_pairs={{0,128},{32,160},{64,192},{96,224},{128,0},{160,32},{192,64},{224,... | collective-permute-start | bytes 3080 | tf_op jit(solution)/shard_map/ppermute | solution.py:625
  49.5 0.4 collective-permute-start.2
  49.9 0.4 collective-permute-start.1
  50.3 0.9 %shard_map.98 = f32[1024,128]{1,0:T(8,128)} custom-call(f32[32,16,128]{2,1,0:T(8,128)S(1)} %get-tuple-element.12.ends, f32[32,48,128]{2,1,0:T(8,128)S(1)} %get-tuple-element.11.kept), custom_call_target="tpu_custom_call" | custom-call | tf_op jit(solution)/shard_map/pallas_call | solution.py:615
  51.2 0.0 collective-permute-done.3
  51.2 0.7 %collective-permute-done.2 = f32[2,128]{1,0:T(2,128)S(1)} collective-permute-done((f32[2,128]{1,0:T(2,128)S(1)}, f32[2,128]{1,0:T(2,128)S(1)}, u32[]{:S(2)}, u32[]{:S(2)}) %collective-permute-start.2) | collective-permute-done | bytes 1056 | tf_op jit(solution)/shard_map/ppermute | solution.py:625
  52.0 1.6 %collective-permute-done.1 = f32[2,128]{1,0:T(2,128)S(1)} collective-permute-done((f32[2,128]{1,0:T(2,128)S(1)}, f32[2,128]{1,0:T(2,128)S(1)}, u32[]{:S(2)}, u32[]{:S(2)}) %collective-permute-start.1) | collective-permute-done | bytes 1056 | tf_op jit(solution)/shard_map/ppermute | solution.py:625
  53.6 0.6 %add_add_fusion = f32[2,128]{1,0:T(2,128)} fusion(f32[2,128]{1,0:T(2,128)S(1)} %collective-permute-done.2, f32[2,128]{1,0:T(2,128)S(1)} %collective-permute-done.3, f32[2,128]{1,0:T(2,128)S(1)} %add.12, f32[2,128]{1,0:T(2,128)S(1)} %collective-permute-done.1), kind=kLoop, calls=%fused_computation | loop fusion | flops 768 | bytes 5120 | tf_op jit(solution)/shard_map/add | solution.py:627
  (1 shorter events, 0.0 us)
Async XLA Ops:
  42.0 4.6 %collective-permute-start = (f32[2,128]{1,0:T(2,128)S(1)}, f32[2,128]{1,0:T(2,128)S(1)}, u32[]{:S(2)}, u32[]{:S(2)}) collective-permute-start(f32[2,128]{1,0:T(2,128)S(1)} %get-tuple-element.13), channel_id=1, source_target_pairs={{0,32},{32,0},{64,96},{96,64},{128,160},{160,128},{192,224},{224,1... | collective-permute-start | bytes 3080 | tf_op jit(solution)/shard_map/ppermute | solution.py:623
  46.6 4.6 %collective-permute-start.3 = (f32[2,128]{1,0:T(2,128)S(1)}, f32[2,128]{1,0:T(2,128)S(1)}, u32[]{:S(2)}, u32[]{:S(2)}) collective-permute-start(f32[2,128]{1,0:T(2,128)S(1)} %add.12), channel_id=1, source_target_pairs={{0,128},{32,160},{64,192},{96,224},{128,0},{160,32},{192,64},{224,... | collective-permute-start | bytes 3080 | tf_op jit(solution)/shard_map/ppermute | solution.py:625
  49.5 2.4 %collective-permute-start.2 = (f32[2,128]{1,0:T(2,128)S(1)}, f32[2,128]{1,0:T(2,128)S(1)}, u32[]{:S(2)}, u32[]{:S(2)}) collective-permute-start(f32[2,128]{1,0:T(2,128)S(1)} %add.12), channel_id=1, source_target_pairs={{0,64},{32,96},{64,0},{96,32},{128,192},{160,224},{192,128},{224,1... | collective-permute-start | bytes 3080 | tf_op jit(solution)/shard_map/ppermute | solution.py:625
  49.9 3.6 %collective-permute-start.1 = (f32[2,128]{1,0:T(2,128)S(1)}, f32[2,128]{1,0:T(2,128)S(1)}, u32[]{:S(2)}, u32[]{:S(2)}) collective-permute-start(f32[2,128]{1,0:T(2,128)S(1)} %add.12), channel_id=1, source_target_pairs={{0,192},{32,224},{64,128},{96,160},{128,64},{160,96},{192,0},{224,... | collective-permute-start | bytes 3080 | tf_op jit(solution)/shard_map/ppermute | solution.py:625
